TPU v7x, 32 devices: a whole 2x2x4 slice. The times are simulated.
32 devices in a mesh: dp: 8 (over z, y), mp: 4 (over x, core).
Axes of the slice: x: 2, y: 2, z: 4, core: 2. Of those that a mesh axis runs over, the one named last changes fastest.
Arguments:
- tokens: bfloat16 [17408, 1024], P(('dp', 'mp')), may hold values from -6 to 6
- caption_len: int32 [8, 2], P('dp'), may hold values from 5 to 64, as said below
- row_offset: int32 [8], P('dp'), may hold values from 0 to 118, as said below
- wqkv: bfloat16 [1024, 3, 1024], P(None, None, 'mp'), may hold values from -0.1875 to 0.1875
- qv_bias: bfloat16 [2, 1024], P(None, 'mp'), may hold values from -1.796875 to 1.796875
- wout: bfloat16 [1024, 1024], P('mp'), may hold values from -0.75 to 0.75
- out_bias: bfloat16 [1024], replicated, may hold values from -0.29882812 to 0.29882812
- w1: bfloat16 [1024, 4096], P(None, 'mp'), may hold values from -0.1875 to 0.1875
- b1: bfloat16 [4096], P('mp'), may hold values from -1.796875 to 1.796875
- w2: bfloat16 [4096, 1024], P('mp'), may hold values from -0.09375 to 0.09375
- b2: bfloat16 [1024], replicated, may hold values from -0.59765625 to 0.59765625
- ln_gain: bfloat16 [4, 1024], replicated, may hold values from 0.5 to 1.5
- ln_bias: bfloat16 [4, 1024], replicated, may hold values from -0.59765625 to 0.59765625
- cotangent: bfloat16 [17408, 1024], P(('dp', 'mp')), may hold values from -6 to 6
Outputs:
- mixed: bfloat16 [17408, 1024], P(('dp', 'mp'))
- tokens_grad: bfloat16 [17408, 1024], P(('dp', 'mp'))
- wqkv_grad: float32 [1024, 3, 1024], P(None, None, 'mp')
- qv_bias_grad: float32 [2, 1024], P(None, 'mp')
- wout_grad: float32 [1024, 1024], P('mp')
- out_bias_grad: float32 [1024], replicated
- w1_grad: float32 [1024, 4096], P(None, 'mp')
- b1_grad: float32 [4096], P('mp')
- w2_grad: float32 [4096, 1024], P('mp')
- b2_grad: float32 [1024], replicated
- ln_gain_grad: float32 [4, 1024], replicated
- ln_bias_grad: float32 [4, 1024], replicated
Inputs may be any that keep to these rules, and one draw needn't show every extreme that they name: `caption_len`: the largest caption length 64 occurs in every draw. A row's items start at row_offset and follow one another without gaps; the last ends at or before position 2176.
All inputs are finite; a program needn't handle non-finite values.
Results may differ from a plain program's by a relative error of at most 0.019.
Values may be sent and summed in bfloat16 or wider, within the bound.
A program may use at most 192 MiB of HBM per device.

v0:
```python
import jax
import jax.numpy as jnp
from jax import lax
from jax.sharding import PartitionSpec as P

HEAD = 64
IMG = 1024


eps_norm = 1e-05
relax_factor = 32.0
masked_value = -1000000000.0


def layer_norm(values, gain, shift):
    center = values - jnp.mean(values, axis=-1, keepdims=True)
    spread = jnp.mean(center * center, axis=-1, keepdims=True)
    return center * lax.rsqrt(spread + eps_norm) * gain + shift


def gelu_tanh(values):
    return jax.nn.gelu(values, approximate=True)


def segment_ids(item_lengths, offset, length):
    ends = offset + jnp.cumsum(item_lengths)
    bounds = jnp.concatenate([jnp.reshape(offset, (1,)), ends])
    place = jnp.arange(length, dtype=jnp.int32)
    return jnp.sum((place[:, None] >= bounds[None, :]).astype(jnp.int32), axis=1)


def row_slice(values, start, count):
    return lax.dynamic_slice_in_dim(values, start, count, 0)


def shards(
    tokens,
    caption_len,
    row_offset,
    wqkv,
    qv_bias,
    wout,
    out_bias,
    w1,
    b1,
    w2,
    b2,
    ln_gain,
    ln_bias,
    cotangent,
):
    local_rows = tokens.shape[0]
    width = tokens.shape[1]
    seq_len = local_rows * lax.axis_size("mp")
    head_part = wqkv.shape[2]
    heads_here = head_part // HEAD
    scale = HEAD ** (-0.5)
    gains = ln_gain.astype(jnp.float32)
    shifts = ln_bias.astype(jnp.float32)
    segment = segment_ids(caption_len[0] + IMG, row_offset[0], seq_len)
    place = jnp.arange(seq_len, dtype=jnp.int32)
    blocks = 4
    qblock = seq_len // blocks
    starts = jnp.arange(blocks, dtype=jnp.int32) * qblock
    rows_in = tokens.astype(jnp.float32)
    norm_a, pull_a = jax.vjp(layer_norm, rows_in, gains[0], shifts[0])
    attn_low = norm_a.astype(jnp.bfloat16)
    attn_full = lax.all_gather(attn_low, "mp", axis=0, tiled=True)
    w_in = wqkv.reshape(width, 3 * head_part)
    projected = jnp.dot(attn_full, w_in, preferred_element_type=jnp.float32).reshape(
        seq_len, 3, heads_here, HEAD
    )
    bias_heads = qv_bias.astype(jnp.float32).reshape(2, heads_here, HEAD)
    queries = (projected[:, 0] + bias_heads[0]).astype(jnp.bfloat16)
    keys_low = projected[:, 1].astype(jnp.bfloat16)
    values_low = (projected[:, 2] + bias_heads[1]).astype(jnp.bfloat16)

    def scores_at(start):
        block_rows = start + jnp.arange(qblock, dtype=jnp.int32)
        block_segment = lax.dynamic_slice_in_dim(segment, start, qblock)
        allowed = (block_segment[:, None] == segment[None, :]) & (
            place[None, :] <= block_rows[:, None]
        )
        query_block = row_slice(queries, start, qblock)
        logits = (
            jnp.einsum("qhd,khd->hqk", query_block, keys_low, preferred_element_type=jnp.float32)
            * scale
        )
        return (query_block, jnp.where(allowed[None], logits, masked_value))

    def forward_block(start):
        query_block, logits = scores_at(start)
        shrunk = logits / relax_factor
        row_top = jnp.max(shrunk, axis=-1, keepdims=True)
        expo = jnp.exp((shrunk - row_top) * relax_factor)
        total = jnp.sum(expo, axis=-1, keepdims=True)
        probs = (expo / total).astype(jnp.bfloat16)
        block_out = jnp.einsum(
            "hqk,khd->qhd", probs, values_low, preferred_element_type=jnp.float32
        )
        return (block_out, (row_top * relax_factor + jnp.log(total))[..., 0])

    head_out, log_totals = lax.map(forward_block, starts)
    head_low = head_out.reshape(seq_len, head_part).astype(jnp.bfloat16)
    attn_out = lax.psum_scatter(
        jnp.dot(
            row_slice(head_low, jnp.int32(0), lax.axis_size("mp") * local_rows),
            wout,
            preferred_element_type=jnp.float32,
        ),
        "mp",
        scatter_dimension=0,
        tiled=True,
    ) + out_bias.astype(jnp.float32)
    norm_b, pull_b = jax.vjp(layer_norm, attn_out, gains[1], shifts[1])
    hidden_rows = rows_in + norm_b
    norm_c, pull_c = jax.vjp(layer_norm, hidden_rows, gains[2], shifts[2])
    mlp_low = norm_c.astype(jnp.bfloat16)
    mlp_full = lax.all_gather(mlp_low, "mp", axis=0, tiled=True)
    pre_act = jnp.dot(mlp_full, w1, preferred_element_type=jnp.float32) + b1.astype(jnp.float32)
    activated, gelu_pull = jax.vjp(gelu_tanh, pre_act)
    act_low = activated.astype(jnp.bfloat16)
    branch = lax.psum_scatter(
        jnp.dot(
            row_slice(act_low, jnp.int32(0), lax.axis_size("mp") * local_rows),
            w2,
            preferred_element_type=jnp.float32,
        ).astype(jnp.bfloat16),
        "mp",
        scatter_dimension=0,
        tiled=True,
    ).astype(jnp.float32)
    branch = branch + b2.astype(jnp.float32)
    norm_d, pull_d = jax.vjp(layer_norm, branch, gains[3], shifts[3])
    mixed = (hidden_rows + norm_d).astype(jnp.bfloat16)
    grad_out = cotangent.astype(jnp.float32)
    grad_branch, gain_d, shift_d = pull_d(grad_out)
    branch_low = grad_branch.astype(jnp.bfloat16)
    b2_part = jnp.sum(branch_low.astype(jnp.float32), axis=0)
    branch_full = lax.all_gather(branch_low, "mp", axis=0, tiled=True)
    w2_grad = jnp.einsum("tf,td->fd", act_low, branch_full, preferred_element_type=jnp.float32)
    grad_act = jnp.einsum("td,fd->tf", branch_full, w2, preferred_element_type=jnp.float32)
    grad_pre = gelu_pull(grad_act)[0].astype(jnp.bfloat16)
    b1_grad = jnp.sum(grad_pre.astype(jnp.float32), axis=0)
    w1_grad = jnp.einsum("td,tf->df", mlp_full, grad_pre, preferred_element_type=jnp.float32)
    grad_norm_c = lax.psum_scatter(
        jnp.einsum(
            "tf,df->td",
            row_slice(grad_pre, jnp.int32(0), lax.axis_size("mp") * local_rows),
            w1,
            preferred_element_type=jnp.float32,
        ).astype(jnp.bfloat16),
        "mp",
        scatter_dimension=0,
        tiled=True,
    ).astype(jnp.float32)
    grad_hidden_c, gain_c, shift_c = pull_c(grad_norm_c)
    grad_hidden = grad_out + grad_hidden_c
    grad_attn, gain_b, shift_b = pull_b(grad_hidden)
    attn_grad_low = grad_attn.astype(jnp.bfloat16)
    out_bias_part = jnp.sum(attn_grad_low.astype(jnp.float32), axis=0)
    attn_grad_full = lax.all_gather(attn_grad_low, "mp", axis=0, tiled=True)
    wout_grad = jnp.einsum(
        "tc,td->cd", head_low, attn_grad_full, preferred_element_type=jnp.float32
    )
    grad_heads = jnp.einsum("td,cd->tc", attn_grad_full, wout, preferred_element_type=jnp.float32)
    grad_heads = grad_heads.astype(jnp.bfloat16).reshape(seq_len, heads_here, HEAD)

    def backward_block(carry, packed):
        key_acc, value_acc = carry
        start, log_total = packed
        query_block, logits = scores_at(start)
        probs = jnp.exp(logits - log_total[..., None])
        grad_block = row_slice(grad_heads, start, qblock)
        grad_probs = jnp.einsum(
            "qhd,khd->hqk", grad_block, values_low, preferred_element_type=jnp.float32
        )
        inner = jnp.sum(probs * grad_probs, axis=-1, keepdims=True)
        grad_logits = (probs * (grad_probs - inner)).astype(jnp.bfloat16)
        value_acc = value_acc + jnp.einsum(
            "hqk,qhd->khd",
            probs.astype(jnp.bfloat16),
            grad_block,
            preferred_element_type=jnp.float32,
        )
        key_acc = (
            key_acc
            + jnp.einsum(
                "hqk,qhd->khd", grad_logits, query_block, preferred_element_type=jnp.float32
            )
            * scale
        )
        grad_query = (
            jnp.einsum("hqk,khd->qhd", grad_logits, keys_low, preferred_element_type=jnp.float32)
            * scale
        )
        return ((key_acc, value_acc), grad_query)

    zero_heads = jnp.zeros((seq_len, heads_here, HEAD), jnp.float32)
    (grad_keys, grad_values), grad_queries = lax.scan(
        backward_block, (zero_heads, zero_heads), (starts, log_totals)
    )
    grad_stack = jnp.stack(
        [grad_queries.reshape(seq_len, heads_here, HEAD), grad_keys, grad_values], axis=1
    )
    grad_proj = grad_stack.astype(jnp.bfloat16).reshape(seq_len, 3 * head_part)
    part_sums = jnp.sum(grad_proj.astype(jnp.float32), axis=0).reshape(3, head_part)
    qv_part = jnp.stack([part_sums[0], part_sums[2]])
    wqkv_grad = jnp.einsum(
        "td,tc->dc", attn_full, grad_proj, preferred_element_type=jnp.float32
    ).reshape(width, 3, head_part)
    grad_norm_a = lax.psum_scatter(
        jnp.einsum(
            "tc,dc->td",
            row_slice(grad_proj, jnp.int32(0), lax.axis_size("mp") * local_rows),
            w_in,
            preferred_element_type=jnp.float32,
        ).astype(jnp.bfloat16),
        "mp",
        scatter_dimension=0,
        tiled=True,
    ).astype(jnp.float32)
    grad_rows_a, gain_a, shift_a = pull_a(grad_norm_a)
    tokens_grad = (grad_hidden + grad_rows_a).astype(jnp.bfloat16)
    wqkv_grad, qv_bias_grad, wout_grad, w1_grad, b1_grad, w2_grad = (
        lax.psum(wqkv_grad.astype(jnp.bfloat16), "dp").astype(jnp.float32),
        lax.psum(qv_part.astype(jnp.bfloat16), "dp").astype(jnp.float32),
        lax.psum(wout_grad.astype(jnp.bfloat16), "dp").astype(jnp.float32),
        lax.psum(w1_grad.astype(jnp.bfloat16), "dp").astype(jnp.float32),
        lax.psum(b1_grad.astype(jnp.bfloat16), "dp").astype(jnp.float32),
        lax.psum(w2_grad.astype(jnp.bfloat16), "dp").astype(jnp.float32),
    )
    gain_stack = jnp.stack([gain_a, gain_b, gain_c, gain_d])
    shift_stack = jnp.stack([shift_a, shift_b, shift_c, shift_d])
    out_bias_grad, b2_grad, ln_gain_grad, ln_bias_grad = lax.psum(
        (out_bias_part, b2_part, gain_stack, shift_stack), ("dp", "mp")
    )
    return (
        mixed,
        tokens_grad,
        wqkv_grad,
        qv_bias_grad,
        wout_grad,
        out_bias_grad,
        w1_grad,
        b1_grad,
        w2_grad,
        b2_grad,
        ln_gain_grad,
        ln_bias_grad,
    )


def solution(mesh):
    placed = (
        P(("dp", "mp"), None),
        P("dp", None),
        P("dp"),
        P(None, None, "mp"),
        P(None, "mp"),
        P("mp", None),
        P(),
        P(None, "mp"),
        P("mp"),
        P("mp", None),
        P(),
        P(),
        P(),
        P(("dp", "mp"), None),
    )
    return jax.shard_map(
        shards,
        mesh=mesh,
        in_specs=placed,
        out_specs=(
            P(("dp", "mp"), None),
            P(("dp", "mp"), None),
            P(None, None, "mp"),
            P(None, "mp"),
            P("mp", None),
            P(),
            P(None, "mp"),
            P("mp"),
            P("mp", None),
            P(),
            P(),
            P(),
        ),
        check_vma=False,
    )
```

profile of v0, /device:TPU:0, one launch (start us, length us, event | category | flops | bytes accessed | tf_op | source)
XLA Modules:
  0.0 1223.7 jit_solution(12304719330502084088)
XLA Ops:
  17.9 35.0 %all-gather.5.cloned.1.call-done = bf16[2176,1024]{1,0:T(8,128)(2,1)} async-done(((bf16[544,1024]{1,0:T(8,128)(2,1)}), bf16[2176,1024]{1,0:T(8,128)(2,1)}) %all-gather.5.cloned.1.call-update) | async-done | bytes 4456464 | tf_op jit(solution)/shard_map/all_gather | solution.py:68
  61.3 141.5 %while.28 = (s32[]{:T(128)}, bf16[4,544,4,64]{1,3,2,0:T(8,128)(2,1)}, f32[4,4,544]{2,1,0:T(4,128)S(1)}, s32[4]{0:T(128)S(1)}, s32[2176]{0:T(1024)S(1)}, /*index=...) while((s32[]{:T(128)}, ...), condition=%wide.region_7.8_spmd.clone, body=%wide.region_4.7_spmd.clone.sunk | while | flops 1296200192 | bytes 153992112 | solution.py:103
  84.7 11.0 fusion.148
  120.0 11.0 fusion.148
  155.3 11.0 fusion.148
  190.5 11.0 fusion.148
  216.6 74.6 %reduce-scatter.5.cloned.1.call-done = f32[544,1024]{1,0:T(8,128)} async-done(((f32[2176,1024]{1,0:T(8,128)}), f32[544,1024]{1,0:T(8,128)}) %reduce-scatter.5.cloned.1.call-update) | async-done | bytes 2228240 | tf_op jit(solution)/shard_map/reduce_scatter | solution.py:105
  297.6 36.1 %all-gather.7.cloned.1.call-done = bf16[2176,1024]{1,0:T(8,128)(2,1)} async-done(((bf16[544,1024]{1,0:T(8,128)(2,1)}), bf16[2176,1024]{1,0:T(8,128)(2,1)}) %all-gather.7.cloned.1.call-update) | async-done | bytes 4456464 | tf_op jit(solution)/shard_map/all_gather | solution.py:119
  352.4 45.6 %reduce-scatter.7.cloned.1.call-done = bf16[544,1024]{1,0:T(8,128)(2,1)} async-done(((bf16[2176,1024]{1,0:T(8,128)(2,1)}), bf16[544,1024]{1,0:T(8,128)(2,1)}) %reduce-scatter.7.cloned.1.call-update) | async-done | bytes 1114128 | tf_op jit(solution)/shard_map/reduce_scatter | solution.py:123
  407.4 36.1 %all-gather.9.cloned.1.call-done = bf16[2176,1024]{1,0:T(8,128)(2,1)} async-done(((bf16[544,1024]{1,0:T(8,128)(2,1)}), bf16[2176,1024]{1,0:T(8,128)(2,1)}) %all-gather.9.cloned.1.call-update) | async-done | bytes 4456464 | tf_op jit(solution)/shard_map/all_gather | solution.py:140
  443.4 14.1 %fusion.86 = (bf16[1024]{0:T(1024)(128)(2,1)}, bf16[2176,1024]{1,0:T(8,128)(2,1)S(1)}) fusion(f32[2176,1024]{1,0:T(8,128)} %copy-done.63, f32[1024]{0:T(1024)S(1)} %convert_element_type.168, bf16[2176,1024]{1,0:T(8,128)(2,1)} %all-gather.9.cloned.1.call-done, bf16[1024,1024]{1,0:T(8,128)(2,1)S(1)} %copy-done), kind=kOutput, calls=%fused_computation.165 | convolution fusion | flops 4612422656 | bytes 19929088 | tf_op jit(solution)/shard_map/td,fd->tf/dot_general | solution.py:142
  466.3 46.1 %reduce-scatter.9.cloned.1.call-done = bf16[544,1024]{1,0:T(8,128)(2,1)} async-done(((bf16[2176,1024]{1,0:T(8,128)(2,1)}), bf16[544,1024]{1,0:T(8,128)(2,1)}) %reduce-scatter.9.cloned.1.call-update) | async-done | bytes 1114128 | tf_op jit(solution)/shard_map/reduce_scatter | solution.py:146
  546.2 16.5 %all-gather.11.cloned.1.call-done = bf16[2176,1024]{1,0:T(8,128)(2,1)} async-done(((bf16[544,1024]{1,0:T(8,128)(2,1)}), bf16[2176,1024]{1,0:T(8,128)(2,1)}) %all-gather.11.cloned.1.call-update) | async-done | bytes 4456464 | tf_op jit(solution)/shard_map/all_gather | solution.py:162
  567.4 323.6 %while.29 = (s32[]{:T(128)}, f32[2176,4,64]{0,2,1:T(8,128)}, f32[2176,4,64]{0,2,1:T(8,128)}, bf16[4,544,4,64]{1,0,3,2:T(4,128)(2,1)}, s32[4]{0:T(128)S(1)}, /*in...) while((s32[]{:T(128)}, f32[2176,4,64]{0,2,1:T(8,128)}, ...), condition=%wide.region_25.26_spmd.clone, body=%wide.region_23.25_spmd.clone.sunk | while | flops 3079612928 | bytes 273078144 | solution.py:200
  582.9 15.0 %multiply_reduce_fusion.7 = (f32[4,544]{1,0:T(4,128)S(1)}, f32[4,544,2176]{2,1,0:T(8,128)}) fusion(f32[4,544,2176]{2,1,0:T(8,128)} %fusion.158, f32[4,544]{1,0:T(4,128)S(1)} %dynamic-slice_bitcast_fusion.2, bf16[2176,4,64]{0,2,1:T(8,128)(2,1)S(1)} %get-tuple-element.477, bf16[2176,4,64]{0,2,1:T(8,128)(2,1)} %get-tuple-element.475, ...), kind=kOutput, calls=%fused_computation.22.clone.1 | convolution fusion | flops 629749632 | bytes 40522756 | tf_op jit(solution)/shard_map/while/body/eval_jaxpr/qhd,khd->hqk/dot_general | solution.py:86
  597.9 16.6 %multiply_convert_fusion.5 = bf16[4,544,2176]{2,1,0:T(8,128)(2,1)} fusion(f32[4,544,2176]{2,1,0:T(8,128)} %get-tuple-element.407, f32[4,544,2176]{2,1,0:T(8,128)} %fusion.158, f32[4,544]{1,0:T(4,128)S(1)} %get-tuple-element.408), kind=kLoop, calls=%fused_computation.21.clone.1 | loop fusion | flops 14204928 | bytes 47358464 | tf_op jit(solution)/shard_map/while/body/eval_jaxpr/convert_element_type | solution.py:179
  634.6 12.7 %dynamic_update_slice.21 = bf16[4,544,4,64]{1,0,3,2:T(4,128)(2,1)} dynamic-update-slice(bf16[4,544,4,64]{1,0,3,2:T(4,128)(2,1)} %get-tuple-element.459, bf16[1,544,4,64]{1,0,3,2:T(2,128)(2,1)S(1)} %copy.62, s32[]{:T(128)S(6)} %copy.79, s32[]{:T(128)} %constant.80.clone.1..sunk.1, s32[]{:T(128)} %constant.80.clone.1..sunk.1, s32[]{:T(128)} %constant.80.clone.1..sunk.1) | dynamic-update-slice | bytes 557060 | tf_op jit(solution)/shard_map/while/body/jit(dynamic_update_index_in_dim)/dynamic_update_slice | solution.py:103
  651.9 10.6 fusion.158
  662.5 15.0 %multiply_reduce_fusion.7 = (f32[4,544]{1,0:T(4,128)S(1)}, f32[4,544,2176]{2,1,0:T(8,128)}) fusion(f32[4,544,2176]{2,1,0:T(8,128)} %fusion.158, f32[4,544]{1,0:T(4,128)S(1)} %dynamic-slice_bitcast_fusion.2, bf16[2176,4,64]{0,2,1:T(8,128)(2,1)S(1)} %get-tuple-element.477, bf16[2176,4,64]{0,2,1:T(8,128)(2,1)} %get-tuple-element.475, ...), kind=kOutput, calls=%fused_computation.22.clone.1 | convolution fusion | flops 629749632 | bytes 40522756 | tf_op jit(solution)/shard_map/while/body/eval_jaxpr/qhd,khd->hqk/dot_general | solution.py:86
  677.5 16.6 %multiply_convert_fusion.5 = bf16[4,544,2176]{2,1,0:T(8,128)(2,1)} fusion(f32[4,544,2176]{2,1,0:T(8,128)} %get-tuple-element.407, f32[4,544,2176]{2,1,0:T(8,128)} %fusion.158, f32[4,544]{1,0:T(4,128)S(1)} %get-tuple-element.408), kind=kLoop, calls=%fused_computation.21.clone.1 | loop fusion | flops 14204928 | bytes 47358464 | tf_op jit(solution)/shard_map/while/body/eval_jaxpr/convert_element_type | solution.py:179
  715.8 12.7 %dynamic_update_slice.21 = bf16[4,544,4,64]{1,0,3,2:T(4,128)(2,1)} dynamic-update-slice(bf16[4,544,4,64]{1,0,3,2:T(4,128)(2,1)} %get-tuple-element.459, bf16[1,544,4,64]{1,0,3,2:T(2,128)(2,1)S(1)} %copy.62, s32[]{:T(128)S(6)} %copy.79, s32[]{:T(128)} %constant.80.clone.1..sunk.1, s32[]{:T(128)} %constant.80.clone.1..sunk.1, s32[]{:T(128)} %constant.80.clone.1..sunk.1) | dynamic-update-slice | bytes 557060 | tf_op jit(solution)/shard_map/while/body/jit(dynamic_update_index_in_dim)/dynamic_update_slice | solution.py:103
  733.1 10.6 fusion.158
  743.7 15.0 %multiply_reduce_fusion.7 = (f32[4,544]{1,0:T(4,128)S(1)}, f32[4,544,2176]{2,1,0:T(8,128)}) fusion(f32[4,544,2176]{2,1,0:T(8,128)} %fusion.158, f32[4,544]{1,0:T(4,128)S(1)} %dynamic-slice_bitcast_fusion.2, bf16[2176,4,64]{0,2,1:T(8,128)(2,1)S(1)} %get-tuple-element.477, bf16[2176,4,64]{0,2,1:T(8,128)(2,1)} %get-tuple-element.475, ...), kind=kOutput, calls=%fused_computation.22.clone.1 | convolution fusion | flops 629749632 | bytes 40522756 | tf_op jit(solution)/shard_map/while/body/eval_jaxpr/qhd,khd->hqk/dot_general | solution.py:86
  758.7 16.6 %multiply_convert_fusion.5 = bf16[4,544,2176]{2,1,0:T(8,128)(2,1)} fusion(f32[4,544,2176]{2,1,0:T(8,128)} %get-tuple-element.407, f32[4,544,2176]{2,1,0:T(8,128)} %fusion.158, f32[4,544]{1,0:T(4,128)S(1)} %get-tuple-element.408), kind=kLoop, calls=%fused_computation.21.clone.1 | loop fusion | flops 14204928 | bytes 47358464 | tf_op jit(solution)/shard_map/while/body/eval_jaxpr/convert_element_type | solution.py:179
  797.0 12.7 %dynamic_update_slice.21 = bf16[4,544,4,64]{1,0,3,2:T(4,128)(2,1)} dynamic-update-slice(bf16[4,544,4,64]{1,0,3,2:T(4,128)(2,1)} %get-tuple-element.459, bf16[1,544,4,64]{1,0,3,2:T(2,128)(2,1)S(1)} %copy.62, s32[]{:T(128)S(6)} %copy.79, s32[]{:T(128)} %constant.80.clone.1..sunk.1, s32[]{:T(128)} %constant.80.clone.1..sunk.1, s32[]{:T(128)} %constant.80.clone.1..sunk.1) | dynamic-update-slice | bytes 557060 | tf_op jit(solution)/shard_map/while/body/jit(dynamic_update_index_in_dim)/dynamic_update_slice | solution.py:103
  824.9 15.0 %multiply_reduce_fusion.7 = (f32[4,544]{1,0:T(4,128)S(1)}, f32[4,544,2176]{2,1,0:T(8,128)}) fusion(f32[4,544,2176]{2,1,0:T(8,128)} %fusion.158, f32[4,544]{1,0:T(4,128)S(1)} %dynamic-slice_bitcast_fusion.2, bf16[2176,4,64]{0,2,1:T(8,128)(2,1)S(1)} %get-tuple-element.477, bf16[2176,4,64]{0,2,1:T(8,128)(2,1)} %get-tuple-element.475, ...), kind=kOutput, calls=%fused_computation.22.clone.1 | convolution fusion | flops 629749632 | bytes 40522756 | tf_op jit(solution)/shard_map/while/body/eval_jaxpr/qhd,khd->hqk/dot_general | solution.py:86
  839.9 16.6 %multiply_convert_fusion.5 = bf16[4,544,2176]{2,1,0:T(8,128)(2,1)} fusion(f32[4,544,2176]{2,1,0:T(8,128)} %get-tuple-element.407, f32[4,544,2176]{2,1,0:T(8,128)} %fusion.158, f32[4,544]{1,0:T(4,128)S(1)} %get-tuple-element.408), kind=kLoop, calls=%fused_computation.21.clone.1 | loop fusion | flops 14204928 | bytes 47358464 | tf_op jit(solution)/shard_map/while/body/eval_jaxpr/convert_element_type | solution.py:179
  878.1 12.7 %dynamic_update_slice.21 = bf16[4,544,4,64]{1,0,3,2:T(4,128)(2,1)} dynamic-update-slice(bf16[4,544,4,64]{1,0,3,2:T(4,128)(2,1)} %get-tuple-element.459, bf16[1,544,4,64]{1,0,3,2:T(2,128)(2,1)S(1)} %copy.62, s32[]{:T(128)S(6)} %copy.79, s32[]{:T(128)} %constant.80.clone.1..sunk.1, s32[]{:T(128)} %constant.80.clone.1..sunk.1, s32[]{:T(128)} %constant.80.clone.1..sunk.1) | dynamic-update-slice | bytes 557060 | tf_op jit(solution)/shard_map/while/body/jit(dynamic_update_index_in_dim)/dynamic_update_slice | solution.py:103
  915.7 22.5 %all-reduce.1 = (bf16[2,256]{1,0:T(2,128)(2,1)S(1)}, bf16[1024]{0:T(1024)(128)(2,1)S(1)}) all-reduce(bf16[2,256]{1,0:T(2,128)(2,1)S(1)} %pad_maximum_fusion.2, bf16[1024]{0:T(1024)(128)(2,1)S(1)} %copy-done.56), channel_id=1, replica_groups=mesh['dp'=8,'mp'=4] {'dp'}, use_global_device_ids=true, to_apply=%region_31.32 | all-reduce | flops 1536 | bytes 6144 | tf_op jit(solution)/shard_map/psum | solution.py:227
  939.4 181.8 %all-reduce.5.cloned.1.call-done = (bf16[1024,3,256]{2,0,1:T(8,128)(2,1)}, bf16[256,1024]{1,0:T(8,128)(2,1)}, bf16[1024,1024]{1,0:T(8,128)(2,1)}, bf16[1024,1024]{1,0:T(8,128)(2,1)}) async-done(((bf16[1024,3,256]{2,0,1:T(8,128)(2,1)}, bf16[256,1024]{1,0:T(8,128)(2,1)}, bf16[1024,1024]{1,0:T(8,128)(2,1)}, bf16[1024,1024]{1,0:T(8,128)(2,1)}), (bf16[1024,3,256]{2,0,1:T(8,128)(2,1)}, ...) | async-done | bytes 6291472 | tf_op jit(solution)/shard_map/psum | solution.py:226
  1131.3 37.7 %reduce-scatter.11.cloned.1.call-done = bf16[544,1024]{1,0:T(8,128)(2,1)} async-done(((bf16[2176,1024]{1,0:T(8,128)(2,1)}), bf16[544,1024]{1,0:T(8,128)(2,1)}) %reduce-scatter.11.cloned.1.call-update) | async-done | bytes 1114128 | tf_op jit(solution)/shard_map/reduce_scatter | solution.py:212
  1172.6 40.4 %all-reduce = (f32[1024]{0:T(1024)}, f32[1024]{0:T(1024)}, f32[4,1024]{1,0:T(4,128)}, f32[4,1024]{1,0:T(4,128)}) all-reduce(f32[1024]{0:T(1024)S(1)} %copy-done.49, f32[1024]{0:T(1024)S(1)} %copy-done.42, f32[4,1024]{1,0:T(4,128)S(1)} %get-tuple-element.283, ...), channel_id=1, replica_groups=mesh['dp'=8,'mp'=4] {'dp','mp'}, use_global_device_ids=true, to_apply=%region_34.35 | all-reduce | flops 10240 | bytes 81920 | tf_op jit(solution)/shard_map/psum | solution.py:235
  (332 shorter events, 362.5 us)
Async XLA Ops:
  7.2 337.2 %copy-start = (bf16[1024,1024]{1,0:T(8,128)(2,1)S(1)}, bf16[1024,1024]{1,0:T(8,128)(2,1)}, u32[]{:S(2)}) copy-start(bf16[1024,1024]{1,0:T(8,128)(2,1)} %param.27) | copy-start | bytes 6291460
  7.2 45.6 %all-gather.5.cloned.1.call-start = ((), (), s32[]{:S(2)}) async-start(), calls=%async_computation.4 | async-start | bytes 5570560 | tf_op jit(solution)/shard_map/all_gather | solution.py:68
  14.0 277.1 %reduce-scatter.5.cloned.1.call-start = ((), (), s32[]{:S(2)}) async-start(), calls=%async_computation.5 | async-start | bytes 11141120 | tf_op jit(solution)/shard_map/reduce_scatter | solution.py:105
  215.9 117.8 %all-gather.7.cloned.1.call-start = ((), (), s32[]{:S(2)}) async-start(), calls=%async_computation.6 | async-start | bytes 5570560 | tf_op jit(solution)/shard_map/all_gather | solution.py:119
  216.5 77.3 %copy-start.37 = (f32[1,1024]{1,0:T(1,128)S(1)}, f32[1,1024]{1,0:T(1,128)}, u32[]{:S(2)}) copy-start(f32[1,1024]{1,0:T(1,128)} %get-tuple-element.273) | copy-start | bytes 12292
  216.6 77.3 %copy-start.52 = (f32[1,1024]{1,0:T(1,128)S(1)}, f32[1,1024]{1,0:T(1,128)}, u32[]{:S(2)}) copy-start(f32[1,1024]{1,0:T(1,128)} %get-tuple-element.277) | copy-start | bytes 12292
  297.6 100.5 %reduce-scatter.7.cloned.1.call-start = ((), (), s32[]{:S(2)}) async-start(), calls=%async_computation.7 | async-start | bytes 5570560 | tf_op jit(solution)/shard_map/reduce_scatter | solution.py:123
  351.7 48.0 %copy-start.34 = (f32[1,1024]{1,0:T(1,128)S(1)}, f32[1,1024]{1,0:T(1,128)}, u32[]{:S(2)}) copy-start(f32[1,1024]{1,0:T(1,128)} %get-tuple-element.271) | copy-start | bytes 12292
  351.8 91.7 %all-gather.9.cloned.1.call-start = ((), (), s32[]{:S(2)}) async-start(), calls=%async_computation.8 | async-start | bytes 5570560 | tf_op jit(solution)/shard_map/all_gather | solution.py:140
  407.3 105.1 %reduce-scatter.9.cloned.1.call-start = ((), (), s32[]{:S(2)}) async-start(), calls=%async_computation.9 | async-start | bytes 5570560 | tf_op jit(solution)/shard_map/reduce_scatter | solution.py:146
  466.1 49.7 %copy-start.14 = (bf16[544,1024]{1,0:T(8,128)(2,1)S(1)}, bf16[544,1024]{1,0:T(8,128)(2,1)}, u32[]{:S(2)}) copy-start(bf16[544,1024]{1,0:T(8,128)(2,1)} %reduce-scatter.7.cloned.1.call-done) | copy-start | bytes 3342340
  466.1 49.7 %copy-start.50 = (f32[1,1024]{1,0:T(1,128)S(1)}, f32[1,1024]{1,0:T(1,128)}, u32[]{:S(2)}) copy-start(f32[1,1024]{1,0:T(1,128)} %get-tuple-element.275) | copy-start | bytes 12292
  466.1 96.6 %all-gather.11.cloned.1.call-start = ((), (), s32[]{:S(2)}) async-start(), calls=%async_computation.10 | async-start | bytes 5570560 | tf_op jit(solution)/shard_map/all_gather | solution.py:162
  526.6 594.6 %all-reduce.5.cloned.1.call-start = ((), (), s32[]{:S(2)}) async-start(), calls=%async_computation.12 | async-start | bytes 12582912 | tf_op jit(solution)/shard_map/psum | solution.py:226
  535.9 26.8 %copy-start.28 = (bf16[256,1024]{1,0:T(8,128)(2,1)S(1)}, bf16[256,1024]{1,0:T(8,128)(2,1)}, u32[]{:S(2)}) copy-start(bf16[256,1024]{1,0:T(8,128)(2,1)} %param.23) | copy-start | bytes 1572868
  677.5 20.6 %copy-start.2 = (f32[4,544,2176]{2,1,0:T(8,128)S(1)}, f32[4,544,2176]{2,1,0:T(8,128)}, u32[]{:S(2)}) copy-start(f32[4,544,2176]{2,1,0:T(8,128)} %get-tuple-element.407) | copy-start | bytes 56819716 | tf_op jit(solution)/shard_map/while
  758.7 20.6 %copy-start.2 = (f32[4,544,2176]{2,1,0:T(8,128)S(1)}, f32[4,544,2176]{2,1,0:T(8,128)}, u32[]{:S(2)}) copy-start(f32[4,544,2176]{2,1,0:T(8,128)} %get-tuple-element.407) | copy-start | bytes 56819716 | tf_op jit(solution)/shard_map/while
  906.3 262.7 %reduce-scatter.11.cloned.1.call-start = ((), (), s32[]{:S(2)}) async-start(), calls=%async_computation.11 | async-start | bytes 5570560 | tf_op jit(solution)/shard_map/reduce_scatter | solution.py:212
  1128.6 40.4 %copy-start.11 = (bf16[544,1024]{1,0:T(8,128)(2,1)S(1)}, bf16[544,1024]{1,0:T(8,128)(2,1)}, u32[]{:S(2)}) copy-start(bf16[544,1024]{1,0:T(8,128)(2,1)} %param.18) | copy-start | bytes 3342340
  1128.6 40.4 %copy-start.30 = (f32[544]{0:T(1024)S(1)}, f32[544]{0:T(1024)}, u32[]{:S(2)}) copy-start(f32[544]{0:T(1024)} %copy-done.29) | copy-start | bytes 6532
  1128.6 40.4 %copy-start.32 = (f32[1,1024]{1,0:T(1,128)S(1)}, f32[1,1024]{1,0:T(1,128)}, u32[]{:S(2)}) copy-start(f32[1,1024]{1,0:T(1,128)} %copy-done.31) | copy-start | bytes 12292
  1131.2 39.9 %copy-start.39 = (f32[544]{0:T(1024)S(1)}, f32[544]{0:T(1024)}, u32[]{:S(2)}) copy-start(f32[544]{0:T(1024)} %copy-done.38) | copy-start | bytes 6532
  1131.2 39.9 %copy-start.36 = (f32[544]{0:T(1024)S(1)}, f32[544]{0:T(1024)}, u32[]{:S(2)}) copy-start(f32[544]{0:T(1024)} %copy-done.35) | copy-start | bytes 6532
  1131.2 41.2 %copy-start.43 = (f32[1024]{0:T(1024)S(1)}, f32[1024]{0:T(1024)}, u32[]{:S(2)}) copy-start(f32[1024]{0:T(1024)} %get-tuple-element.200) | copy-start | bytes 12292
  1131.2 41.2 %copy-start.44 = (f32[1024]{0:T(1024)S(1)}, f32[1024]{0:T(1024)}, u32[]{:S(2)}) copy-start(f32[1024]{0:T(1024)} %get-tuple-element.189) | copy-start | bytes 12292
  1131.2 41.2 %copy-start.45 = (f32[1024]{0:T(1024)S(1)}, f32[1024]{0:T(1024)}, u32[]{:S(2)}) copy-start(f32[1024]{0:T(1024)} %get-tuple-element.198) | copy-start | bytes 12292
  1131.3 41.2 %copy-start.46 = (f32[1024]{0:T(1024)S(1)}, f32[1024]{0:T(1024)}, u32[]{:S(2)}) copy-start(f32[1024]{0:T(1024)} %get-tuple-element.187) | copy-start | bytes 12292
  1131.3 41.2 %copy-start.47 = (f32[1024]{0:T(1024)S(1)}, f32[1024]{0:T(1024)}, u32[]{:S(2)}) copy-start(f32[1024]{0:T(1024)} %get-tuple-element.185) | copy-start | bytes 12292
  1131.3 41.2 %copy-start.48 = (f32[1024]{0:T(1024)S(1)}, f32[1024]{0:T(1024)}, u32[]{:S(2)}) copy-start(f32[1024]{0:T(1024)} %get-tuple-element.193) | copy-start | bytes 12292
  1131.3 41.2 %copy-start.42 = (f32[1024]{0:T(1024)S(1)}, f32[1024]{0:T(1024)}, u32[]{:S(2)}) copy-start(f32[1024]{0:T(1024)} %get-tuple-element.251) | copy-start | bytes 12292
  1131.3 41.2 %copy-start.49 = (f32[1024]{0:T(1024)S(1)}, f32[1024]{0:T(1024)}, u32[]{:S(2)}) copy-start(f32[1024]{0:T(1024)} %get-tuple-element.253) | copy-start | bytes 12292
  1172.5 44.1 %copy-start.1 = (bf16[1024,1024]{1,0:T(8,128)(2,1)S(1)}, bf16[1024,1024]{1,0:T(8,128)(2,1)}, u32[]{:S(2)}) copy-start(bf16[1024,1024]{1,0:T(8,128)(2,1)} %param.27) | copy-start | bytes 6291460
  (59 other events, 269.9 us)
Sparse Core Ops, SparseCore 0:
  14.1 38.7 all-gather.4
  216.0 75.0 reduce-scatter.4
  297.7 35.9 all-gather.6
  351.9 46.1 reduce-scatter.6
  407.4 35.9 all-gather.8
  466.2 46.1 reduce-scatter.8
  526.7 35.9 all-gather.10
  906.5 214.6 all-reduce.4
  1123.9 45.0 reduce-scatter.10
where the time goes:
time: 1230 us; the launch traced here: 1220 us
  waiting for transfers between devices  510 us (41%)
  matrix products  322 us (26%)
  other arithmetic  164 us (13%)
  local copies, waits for them, and re-layouts  132 us (11%)
  blocking collectives  62.9 us (5%)
  loops' own time  16.8 us (1%)
  between operations  15.5 us (1%)
    psum x1, waiting for transfers between devices, shards(): lax.psum(wqkv_grad.astype(jnp.bfloat16), 'dp').astype(jnp.float32)  182 us
    dot_general x8, matrix products, scores_at(): jnp.einsum('qhd,khd->hqk', query_block, keys_low, preferred_element_type=...  82.4 us
    reduce_scatter x1, waiting for transfers between devices, shards(): lax.psum_scatter(jnp.dot(row_slice(head_low, jnp.int32(0), lax.axis_size(...  74.6 us
    convert_element_type x4, other arithmetic, backward_block(): grad_logits = (probs * (grad_probs - inner)).astype(jnp.bfloat16)  66.4 us
    dynamic_update_slice x8, local copies, waits for them, and re-layouts, shards(): head_out, log_totals = lax.map(forward_block, starts)  52.8 us
    while x48, local copies, waits for them, and re-layouts  46.2 us
    reduce_scatter x1, waiting for transfers between devices, shards(): lax.psum_scatter(jnp.einsum('tf,df->td', row_slice(grad_pre, jnp.int32(0)...  46.1 us
    reduce_scatter x1, waiting for transfers between devices, shards(): lax.psum_scatter(jnp.dot(row_slice(act_low, jnp.int32(0), lax.axis_size('...  45.6 us
  transfers between devices with their start and end apart: 9, of which 9 were waited for; matrix products, arithmetic and copies ran while one was open for 3% of the time, Pallas kernels for 0%

commit v1 on v0

v1 whole, which is shorter than its diff:
```python
import functools
import jax, jax.numpy as jnp
from jax import lax
from jax.experimental import pallas as pl
from jax.experimental.pallas import tpu as pltpu
from jax.sharding import PartitionSpec as P
HEAD=64; IMG=1024; CAP_MIN=5; LANES=128
F32=jnp.float32; BF=jnp.bfloat16
NT=(((1,),(1,)),((),()))
TN=(((0,),(0,)),((),()))

def plan(seq):
    least=IMG+CAP_MIN
    slack=seq-2*least
    lo=least//LANES*LANES
    hi=-(-(seq-least)//LANES)*LANES
    head_pad=-(-slack//LANES)*LANES
    tail_pad=(2*least)//LANES*LANES
    def cut(a,b,step):
        out=[]
        while a<b:
            out.append((a,min(a+step,b))); a=min(a+step,b)
        return out
    return lo,hi,head_pad,tail_pad,cut

def free_of_mask(k0,k1,q0,q1,seq):
    lo,hi,head_pad,tail_pad,_=plan(seq)
    if k1>q0: return False
    if q1<=lo: return k0>=head_pad
    if q0>=hi: return k0>=hi and q1<=tail_pad
    return False

def seg_start(pos,b0,b1,b2):
    return jnp.where(pos>=b2,b2,jnp.where(pos>=b1,b1,jnp.where(pos>=b0,b0,0)))

def fwd_kernel(bounds,q_ref,k_ref,v_ref,o_ref,lse_ref):
    seq,width=q_ref.shape
    h=pl.program_id(0)
    b0,b1,b2=bounds[0],bounds[1],bounds[2]
    lo,hi,_,_,cut=plan(seq)
    lane=lax.broadcasted_iota(jnp.int32,(1,width),1)
    mine=(lane//HEAD)==h
    blocks=[(a,b,0) for a,b in cut(0,lo,256)]+[(a,b,0) for a,b in cut(lo,hi,256)]+[(a,b,lo) for a,b in cut(hi,seq,256)]
    for a,b,start in blocks:
        n=b-a
        qm=jnp.where(mine,q_ref[a:b,:].astype(F32)*HEAD**-0.5,0.0).astype(BF)
        qpos=a+lax.broadcasted_iota(jnp.int32,(n,1),0)
        first=seg_start(qpos,b0,b1,b2)
        parts=[]
        top=None
        for c,d in cut(start,b,128):
            s=lax.dot_general(qm,k_ref[c:d,:],NT,preferred_element_type=F32)
            if not free_of_mask(c,d,a,b,seq):
                kpos=c+lax.broadcasted_iota(jnp.int32,(n,d-c),1)
                s=jnp.where((kpos>=first)&(kpos<=qpos),s,-1e9)
            parts.append(s)
            top=s if top is None else jnp.maximum(top,s)
        m=jnp.max(top,axis=1,keepdims=True)
        es=[jnp.exp(s-m) for s in parts]
        tot=es[0]
        for e in es[1:]: tot=tot+e
        l=jnp.sum(tot,axis=1,keepdims=True)
        p=jnp.concatenate([e.astype(BF) for e in es],axis=1)
        o=jnp.dot(p,v_ref[start:b,:],preferred_element_type=F32)/l
        o_ref[a:b,:]=jnp.where(mine,o.astype(BF),o_ref[a:b,:])
        lse=m+jnp.log(l)
        lse_ref[0,:,a:b]=jnp.broadcast_to(lse,(n,128)).T[0:8,:]

def bwd_kernel(bounds,q_ref,k_ref,v_ref,o_ref,do_ref,lse_ref,dq_ref,dk_ref,dv_ref,qm_s,dom_s,dqt_s,delta_s):
    seq,width=q_ref.shape
    h=pl.program_id(0)
    b0,b1,b2=bounds[0],bounds[1],bounds[2]
    lo,hi,_,_,cut=plan(seq)
    lane=lax.broadcasted_iota(jnp.int32,(1,width),1)
    mine=(lane//HEAD)==h
    qm_s[...]=jnp.where(mine,q_ref[...].astype(F32)*HEAD**-0.5,0.0).astype(BF)
    dom_s[...]=jnp.where(mine,do_ref[...],jnp.zeros((),BF))
    ones=jnp.ones((8,width),F32)
    for a,b in cut(0,seq,256):
        prod=dom_s[a:b,:].astype(F32)*o_ref[a:b,:].astype(F32)
        delta_s[:,a:b]=lax.dot_general(ones,prod,NT,preferred_element_type=F32,precision=lax.Precision.HIGHEST)
    dqt_s[...]=jnp.zeros_like(dqt_s)
    blocks=[(a,b,hi) for a,b in cut(0,lo,256)]+[(a,b,seq) for a,b in cut(lo,hi,256)]+[(a,b,seq) for a,b in cut(hi,seq,256)]
    for a,b,stop in blocks:
        n=b-a
        kk=k_ref[a:b,:]; vv=v_ref[a:b,:]
        kpos=a+lax.broadcasted_iota(jnp.int32,(n,1),0)
        kh=jnp.where(mine,kk,jnp.zeros((),BF))
        pts=[];dsts=[]
        for c,d in cut(a,stop,128):
            st=lax.dot_general(kk,qm_s[c:d,:],NT,preferred_element_type=F32)
            pt=jnp.exp(st-lse_ref[0,0:1,c:d])
            if not free_of_mask(a,b,c,d,seq):
                qpos=c+lax.broadcasted_iota(jnp.int32,(1,d-c),1)
                first=seg_start(qpos,b0,b1,b2)
                pt=jnp.where((kpos>=first)&(kpos<=qpos),pt,0.0)
            dpt=lax.dot_general(vv,dom_s[c:d,:],NT,preferred_element_type=F32)
            dst=pt*(dpt-delta_s[0:1,c:d])
            pts.append(pt.astype(BF)); dsts.append(dst.astype(BF))
        pt=jnp.concatenate(pts,axis=1); dst=jnp.concatenate(dsts,axis=1)
        dv=jnp.dot(pt,dom_s[a:stop,:],preferred_element_type=F32)
        dk=jnp.dot(dst,qm_s[a:stop,:],preferred_element_type=F32)
        dv_ref[a:b,:]=jnp.where(mine,dv.astype(BF),dv_ref[a:b,:])
        dk_ref[a:b,:]=jnp.where(mine,dk.astype(BF),dk_ref[a:b,:])
        dqt_s[:,a:stop]+=lax.dot_general(kh,dst,TN,preferred_element_type=F32)
    for a,b in cut(0,seq,128):
        dq=(dqt_s[:,a:b]*HEAD**-0.5).T
        dq_ref[a:b,:]=jnp.where(mine,dq.astype(BF),dq_ref[a:b,:])

def attn_fwd(bounds,q,k,v):
    seq,width=q.shape; H=width//HEAD
    full=pl.BlockSpec((seq,width),lambda h:(0,0))
    return pl.pallas_call(fwd_kernel,grid=(H,),
        in_specs=[pl.BlockSpec(memory_space=pltpu.SMEM),full,full,full],
        out_specs=[full,pl.BlockSpec((1,8,seq),lambda h:(h,0,0))],
        out_shape=[jax.ShapeDtypeStruct((seq,width),BF),jax.ShapeDtypeStruct((H,8,seq),F32)],
        compiler_params=pltpu.CompilerParams(vmem_limit_bytes=56<<20),name="attn_fwd")(bounds,q,k,v)

def attn_bwd(bounds,q,k,v,o,do,lse):
    seq,width=q.shape; H=width//HEAD
    full=pl.BlockSpec((seq,width),lambda h:(0,0))
    sh=jax.ShapeDtypeStruct((seq,width),BF)
    return pl.pallas_call(bwd_kernel,grid=(H,),
        in_specs=[pl.BlockSpec(memory_space=pltpu.SMEM),full,full,full,full,full,pl.BlockSpec((1,8,seq),lambda h:(h,0,0))],
        out_specs=[full,full,full],out_shape=[sh,sh,sh],
        scratch_shapes=[pltpu.VMEM((seq,width),BF),pltpu.VMEM((seq,width),BF),pltpu.VMEM((width,seq),F32),pltpu.VMEM((8,seq),F32)],
        compiler_params=pltpu.CompilerParams(vmem_limit_bytes=56<<20),name="attn_bwd")(bounds,q,k,v,o,do,lse)

eps_norm = 1e-05


def layer_norm(values, gain, shift):
    center = values - jnp.mean(values, axis=-1, keepdims=True)
    spread = jnp.mean(center * center, axis=-1, keepdims=True)
    return center * lax.rsqrt(spread + eps_norm) * gain + shift


def gelu_tanh(values):
    return jax.nn.gelu(values, approximate=True)


def swap(values, axis, mask):
    size = lax.axis_size(axis)
    return lax.ppermute(values, axis, [(i, i ^ mask) for i in range(size)])


def masks_of(axis):
    size = lax.axis_size(axis)
    out = []
    step = size // 2
    while step:
        out.append(step)
        step //= 2
    return out


def gather_rel(block, axis):
    have = {0: block}
    for mask in masks_of(axis):
        have.update({j ^ mask: swap(v, axis, mask) for j, v in list(have.items())})
    return jnp.stack([have[j] for j in range(lax.axis_size(axis))])


def scatter_rel(parts, axis):
    have = {j: parts[j] for j in range(parts.shape[0])}
    for mask in reversed(masks_of(axis)):
        got = {j: swap(have[j].astype(BF), axis, mask) for j in have if j & mask}
        have = {j: have[j] + got[j ^ mask].astype(F32) for j in have if not j & mask}
    return have[0]


def reduce_all(values, axis):
    me = lax.axis_index(axis)
    masks = list(reversed(masks_of(axis)))
    rows = values.shape[0]
    for mask in masks:
        rows //= 2
        bit = (me // mask) % 2
        keep = lax.dynamic_slice_in_dim(values, bit * rows, rows, 0)
        send = lax.dynamic_slice_in_dim(values, (1 - bit) * rows, rows, 0)
        values = keep + swap(send.astype(BF), axis, mask).astype(F32)
    low = values.astype(BF)
    for mask in reversed(masks):
        bit = (me // mask) % 2
        got = swap(low, axis, mask)
        both = jnp.concatenate([low, got], axis=0)
        flipped = jnp.concatenate([got, low], axis=0)
        low = jnp.where(bit == 0, both, flipped)
    return low.astype(F32)


def sum_small(values, axes):
    for axis in axes:
        for mask in masks_of(axis):
            values = values + swap(values, axis, mask)
    return values


def shards(
    tokens, caption_len, row_offset, wqkv, qv_bias, wout, out_bias, w1, b1, w2, b2, ln_gain, ln_bias, cotangent,
):
    local_rows, width = tokens.shape
    size = lax.axis_size("mp")
    seq_len = local_rows * size
    head_part = wqkv.shape[2]
    gains = ln_gain.astype(F32)
    shifts = ln_bias.astype(F32)
    me = lax.axis_index("mp")

    def pick(blocks):
        return jnp.concatenate(
            [lax.dynamic_index_in_dim(blocks, me ^ j, 0, keepdims=True) for j in range(size)], axis=0
        )

    first = row_offset[0]
    second = first + caption_len[0, 0] + IMG
    third = second + caption_len[0, 1] + IMG
    bounds = jnp.stack([first, second, third]).astype(jnp.int32)

    def sort(rel):
        return pick(rel).reshape((seq_len,) + rel.shape[2:])

    def rel_of(rows):
        return pick(rows.reshape((size, local_rows) + rows.shape[1:]))

    rows_in = tokens.astype(F32)
    norm_a, pull_a = jax.vjp(layer_norm, rows_in, gains[0], shifts[0])
    attn_full = sort(gather_rel(norm_a.astype(BF), "mp"))
    w_in = wqkv.reshape(width, 3 * head_part)
    projected = jnp.dot(attn_full, w_in, preferred_element_type=F32)
    bias3 = jnp.concatenate([qv_bias[0], jnp.zeros_like(qv_bias[0]), qv_bias[1]]).astype(F32)
    projected = (projected + bias3).astype(BF)
    queries, keys, values = [projected[:, i * head_part:(i + 1) * head_part] for i in range(3)]
    head_low, lse = attn_fwd(bounds, queries, keys, values)
    head_rel = rel_of(head_low)
    attn_out = scatter_rel(jnp.dot(head_rel, wout, preferred_element_type=F32), "mp") + out_bias.astype(F32)
    norm_b, pull_b = jax.vjp(layer_norm, attn_out, gains[1], shifts[1])
    hidden_rows = rows_in + norm_b
    norm_c, pull_c = jax.vjp(layer_norm, hidden_rows, gains[2], shifts[2])
    mlp_rel = gather_rel(norm_c.astype(BF), "mp")
    mlp_full = mlp_rel.reshape(seq_len, width)
    pre_act = jnp.dot(mlp_full, w1, preferred_element_type=F32) + b1.astype(F32)
    activated, gelu_pull = jax.vjp(gelu_tanh, pre_act)
    act_low = activated.astype(BF)
    branch = scatter_rel(
        jnp.dot(act_low, w2, preferred_element_type=F32).reshape(size, local_rows, width), "mp"
    ) + b2.astype(F32)
    norm_d, pull_d = jax.vjp(layer_norm, branch, gains[3], shifts[3])
    mixed = (hidden_rows + norm_d).astype(BF)
    grad_out = cotangent.astype(F32)
    grad_branch, gain_d, shift_d = pull_d(grad_out)
    branch_low = grad_branch.astype(BF)
    b2_part = jnp.sum(branch_low.astype(F32), axis=0)
    branch_full = gather_rel(branch_low, "mp").reshape(seq_len, width)
    w2_grad = jnp.einsum("tf,td->fd", act_low, branch_full, preferred_element_type=F32)
    w2_grad = reduce_all(w2_grad, "dp")
    grad_act = jnp.einsum("td,fd->tf", branch_full, w2, preferred_element_type=F32)
    grad_pre = gelu_pull(grad_act)[0].astype(BF)
    b1_grad = jnp.sum(grad_pre.astype(F32), axis=0)
    w1_grad = jnp.einsum("td,tf->df", mlp_full, grad_pre, preferred_element_type=F32)
    w1_grad = reduce_all(w1_grad, "dp")
    grad_norm_c = scatter_rel(
        jnp.einsum("tf,df->td", grad_pre, w1, preferred_element_type=F32).reshape(size, local_rows, width), "mp"
    )
    grad_hidden_c, gain_c, shift_c = pull_c(grad_norm_c)
    grad_hidden = grad_out + grad_hidden_c
    grad_attn, gain_b, shift_b = pull_b(grad_hidden)
    attn_grad_low = grad_attn.astype(BF)
    out_bias_part = jnp.sum(attn_grad_low.astype(F32), axis=0)
    attn_grad_full = sort(gather_rel(attn_grad_low, "mp"))
    wout_grad = jnp.einsum("tc,td->cd", head_low, attn_grad_full, preferred_element_type=F32)
    wout_grad = reduce_all(wout_grad, "dp")
    grad_heads = jnp.einsum("td,cd->tc", attn_grad_full, wout, preferred_element_type=F32).astype(BF)
    grads = attn_bwd(bounds, queries, keys, values, head_low, grad_heads, lse)
    grad_proj = jnp.concatenate(grads, axis=1)
    part_sums = jnp.sum(grad_proj.astype(F32), axis=0).reshape(3, head_part)
    qv_part = jnp.stack([part_sums[0], part_sums[2]])
    wqkv_grad = jnp.einsum("td,tc->dc", attn_full, grad_proj, preferred_element_type=F32)
    wqkv_grad = reduce_all(wqkv_grad, "dp").reshape(width, 3, head_part)
    grad_rel = rel_of(grad_proj)
    grad_norm_a = scatter_rel(jnp.einsum("jtc,dc->jtd", grad_rel, w_in, preferred_element_type=F32), "mp")
    grad_rows_a, gain_a, shift_a = pull_a(grad_norm_a)
    tokens_grad = (grad_hidden + grad_rows_a).astype(BF)
    own_sums = sum_small(jnp.concatenate([qv_part.reshape(-1), b1_grad]), ("dp",))
    qv_sum = own_sums[: 2 * head_part].reshape(2, head_part)
    b1_sum = own_sums[2 * head_part:]
    stack = jnp.stack(
        [gain_a, gain_b, gain_c, gain_d, shift_a, shift_b, shift_c, shift_d, out_bias_part, b2_part]
    )
    stack = sum_small(stack, ("mp", "dp"))
    return (
        mixed, tokens_grad, wqkv_grad, qv_sum, wout_grad, stack[8], w1_grad, b1_sum, w2_grad, stack[9],
        stack[0:4], stack[4:8],
    )


def solution(mesh):
    rows = P(("dp", "mp"), None)
    placed = (
        rows, P("dp", None), P("dp"), P(None, None, "mp"), P(None, "mp"), P("mp", None), P(), P(None, "mp"),
        P("mp"), P("mp", None), P(), P(), P(), rows,
    )
    return jax.shard_map(
        shards,
        mesh=mesh,
        in_specs=placed,
        out_specs=(
            rows, rows, P(None, None, "mp"), P(None, "mp"), P("mp", None), P(), P(None, "mp"), P("mp"),
            P("mp", None), P(), P(), P(),
        ),
        check_vma=False,
    )
```

time: 1230 us -> 569 us (0.46)
  waiting for transfers between devices: 510 us -> 246 us
  matrix products: 322 us -> 61.4 us
  local copies, waits for them, and re-layouts: 132 us -> 39.4 us
  other arithmetic: 164 us -> 94.8 us
  blocking collectives: 62.9 us -> 0 us
  Pallas kernels: 0 us -> 60.6 us
  starting transfers between devices: 1.01 us -> 54.7 us
  loops' own time: 16.8 us -> 0 us
    dot_general x39 -> x11, matrix products: 320 us -> 59.1 us  [the longest x1 12.5 us: shards(): jnp.einsum('td,fd->tf', branch_full, w2, preferred_element_type=F32)]
    ppermute x0 -> x56, waiting for transfers between devices: none -> 246 us  [swap(): return lax.ppermute(values, axis, [(i, i ^ mask) for i in range(size)])]
    reduce_scatter x4 -> x0, waiting for transfers between devices: 204 us -> none  [the longest x1 74.6 us: shards(): lax.psum_scatter(jnp.dot(row_slice(head_low, jnp.int32(0), lax.axis_size(...]
    psum x1 -> x0, waiting for transfers between devices: 182 us -> none  [shards(): lax.psum(wqkv_grad.astype(jnp.bfloat16), 'dp').astype(jnp.float32)]
    all_gather x4 -> x0, waiting for transfers between devices: 124 us -> none  [the longest x1 36.1 us: shards(): branch_full = lax.all_gather(branch_low, 'mp', axis=0, tiled=True)]
    psum x2 -> x0, blocking collectives: 62.9 us -> none  [the longest x1 40.4 us: shards(): lax.psum((out_bias_part, b2_part, gain_stack, shift_stack), ('dp', 'mp'))]
    pallas_call x0 -> x2, Pallas kernels: none -> 60.6 us  [the longest x1 38.4 us: attn_bwd(): pl.pallas_call(bwd_kernel, grid=(H,), in_specs=[pl.BlockSpec(memory_space...]
    convert_element_type x18 -> x19, other arithmetic: 85.4 us -> 28.9 us  [the longest x4 16.1 us: reduce_all(): return low.astype(F32)]
  transfers between devices with their start and end apart: 9 -> 56, of which waited for: 9 -> 27; matrix products, arithmetic and copies ran while one was open for 3% -> 23% of each run, Pallas kernels for 0% -> 7%
where the time goes in v1:
time: 569 us; the launch traced here: 561 us
  waiting for transfers between devices  246 us (43%)
  other arithmetic  94.8 us (17%)
  matrix products  61.4 us (11%)
  Pallas kernels  60.6 us (11%)
  starting transfers between devices  54.7 us (10%)
  local copies, waits for them, and re-layouts  39.4 us (7%)
    ppermute x56, waiting for transfers between devices, swap(): return lax.ppermute(values, axis, [(i, i ^ mask) for i in range(size)])  246 us
    ppermute x56, starting transfers between devices, swap(): return lax.ppermute(values, axis, [(i, i ^ mask) for i in range(size)])  54.7 us
    pallas_call x1, Pallas kernels, attn_bwd(): pl.pallas_call(bwd_kernel, grid=(H,), in_specs=[pl.BlockSpec(memory_space...  38.4 us
    pallas_call x1, Pallas kernels, attn_fwd(): pl.pallas_call(fwd_kernel, grid=(H,), in_specs=[pl.BlockSpec(memory_space...  22.3 us
    select_n x10, other arithmetic, reduce_all(): low = jnp.where(bit == 0, both, flipped)  19.9 us
    convert_element_type x4, other arithmetic, reduce_all(): return low.astype(F32)  16.1 us
    reduce_sum x5, other arithmetic, layer_norm(): return center * lax.rsqrt(spread + eps_norm) * gain + shift  14.8 us
    unnamed x112, local copies, waits for them, and re-layouts  13.3 us
  transfers between devices with their start and end apart: 56, of which 27 were waited for; matrix products, arithmetic and copies ran while one was open for 23% of the time, Pallas kernels for 7%

profile of v1, /device:TPU:0, one launch (start us, length us, event | category | flops | bytes accessed | tf_op | source)
XLA Modules:
  0.0 561.2 jit_solution(13439972681696496398)
XLA Ops:
  9.2 24.9 %collective-permute-done.1 = bf16[544,1024]{1,0:T(8,128)(2,1)} collective-permute-done((bf16[544,1024]{1,0:T(8,128)(2,1)}, bf16[544,1024]{1,0:T(8,128)(2,1)}, u32[]{:S(2)}, u32[]{:S(2)}) %collective-permute-start.1) | collective-permute-done | bytes 1114144 | tf_op jit(solution)/shard_map/ppermute | solution.py:144
  44.5 3.9 add_convert_fusion
  50.2 22.3 %attn_fwd.1 = (bf16[2176,256]{1,0:T(8,128)(2,1)}, f32[4,8,2176]{2,1,0:T(8,128)}) custom-call(s32[3]{0:T(128)} %pad_add_fusion.bounds, bf16[2176,256]{1,0:T(8,128)(2,1)} %get-tuple-element.80.q_ref, bf16[2176,256]{1,0:T(8,128)(2,1)} %get-tuple-element.79.k_ref, bf16[2176,256]{1,0:T(8,128)(2,1)} %get-tuple-element.78.v_ref), custom_call_target="tpu_custom_call" | custom-call | tf_op jit(solution)/shard_map/attn_fwd/pallas_call | solution.py:113
  80.6 25.1 %collective-permute-done.5 = bf16[544,1024]{1,0:T(8,128)(2,1)S(1)} collective-permute-done((bf16[544,1024]{1,0:T(8,128)(2,1)S(1)}, bf16[544,1024]{1,0:T(8,128)(2,1)S(1)}, u32[]{:S(2)}, u32[]{:S(2)}) %collective-permute-start.5) | collective-permute-done | bytes 1114144 | tf_op jit(solution)/shard_map/ppermute | solution.py:144
  110.2 24.3 %collective-permute-done.7 = bf16[544,1024]{1,0:T(8,128)(2,1)S(1)} collective-permute-done((bf16[544,1024]{1,0:T(8,128)(2,1)S(1)}, bf16[544,1024]{1,0:T(8,128)(2,1)S(1)}, u32[]{:S(2)}, u32[]{:S(2)}) %collective-permute-start.7) | collective-permute-done | bytes 1114144 | tf_op jit(solution)/shard_map/ppermute | solution.py:144
  137.8 9.4 %multiply_convert_fusion = (bf16[2176,1024]{1,0:T(8,128)(2,1)S(1)}, f32[2176,1024]{1,0:T(8,128)}) fusion(f32[1024]{0:T(1024)S(1)} %convert_element_type.249, bf16[2176,1024]{1,0:T(8,128)(2,1)S(1)} %bitcast.132, bf16[1024,1024]{1,0:T(8,128)(2,1)S(1)} %copy-done), kind=kOutput, calls=%fused_computation.10 | convolution fusion | flops 4585684992 | bytes 19927040 | tf_op jit(solution)/shard_map/dot_general | solution.py:242
  147.2 4.8 fusion.87
  157.3 24.9 %collective-permute-done.11 = bf16[544,1024]{1,0:T(8,128)(2,1)S(1)} collective-permute-done((bf16[544,1024]{1,0:T(8,128)(2,1)S(1)}, bf16[544,1024]{1,0:T(8,128)(2,1)S(1)}, u32[]{:S(2)}, u32[]{:S(2)}) %collective-permute-start.11) | collective-permute-done | bytes 1114144 | tf_op jit(solution)/shard_map/ppermute | solution.py:144
  190.0 24.1 %collective-permute-done.13 = bf16[544,1024]{1,0:T(8,128)(2,1)} collective-permute-done((bf16[544,1024]{1,0:T(8,128)(2,1)S(1)}, bf16[544,1024]{1,0:T(8,128)(2,1)}, u32[]{:S(2)}, u32[]{:S(2)}) %collective-permute-start.13) | collective-permute-done | bytes 1114144 | tf_op jit(solution)/shard_map/ppermute | solution.py:144
  219.5 7.0 %fusion.93 = f32[1024,1024]{1,0:T(8,128)S(1)} fusion(bf16[2176,1024]{1,0:T(8,128)(2,1)} %copy-done.49, bf16[2176,1024]{1,0:T(8,128)(2,1)S(1)} %bitcast.136), kind=kOutput, calls=%fused_computation.217 | convolution fusion | flops 4563402752 | bytes 13107200 | tf_op jit(solution)/shard_map/tf,td->fd/dot_general | solution.py:255
  231.5 12.5 %convert_reduce_fusion = (f32[1024]{0:T(1024)S(1)}, bf16[2176,1024]{1,0:T(8,128)(2,1)S(1)}) fusion(f32[2176,1024]{1,0:T(8,128)} %get-tuple-element.105, f32[1024]{0:T(1024)S(1)} %convert_element_type.249, bf16[2176,1024]{1,0:T(8,128)(2,1)S(1)} %bitcast.137, bf16[1024,1024]{1,0:T(8,128)(2,1)S(1)} %copy-done.48), kind=kOutput, calls=%fused_computation.9 | convolution fusion | flops 4614650880 | bytes 19931136 | tf_op jit(solution)/shard_map/td,fd->tf/dot_general | solution.py:257
  244.0 4.8 fusion.88
  249.2 5.3 fusion.92
  264.3 17.3 %collective-permute-done.44 = bf16[512,1024]{1,0:T(8,128)(2,1)} collective-permute-done((bf16[512,1024]{1,0:T(8,128)(2,1)}, bf16[512,1024]{1,0:T(8,128)(2,1)}, u32[]{:S(2)}, u32[]{:S(2)}) %collective-permute-start.44) | collective-permute-done | bytes 1048608 | tf_op jit(solution)/shard_map/ppermute | solution.py:144
  305.3 13.4 %collective-permute-done.52 = bf16[128,1024]{1,0:T(8,128)(2,1)} collective-permute-done((bf16[128,1024]{1,0:T(8,128)(2,1)}, bf16[128,1024]{1,0:T(8,128)(2,1)}, u32[]{:S(2)}, u32[]{:S(2)}) %collective-permute-start.52) | collective-permute-done | bytes 262176 | tf_op jit(solution)/shard_map/ppermute | solution.py:144
  321.0 8.7 %collective-permute-done.46 = bf16[128,1024]{1,0:T(8,128)(2,1)} collective-permute-done((bf16[128,1024]{1,0:T(8,128)(2,1)}, bf16[128,1024]{1,0:T(8,128)(2,1)}, u32[]{:S(2)}, u32[]{:S(2)}) %collective-permute-start.46) | collective-permute-done | bytes 262176 | tf_op jit(solution)/shard_map/ppermute | solution.py:144
  337.5 6.2 %collective-permute-start.54 = (bf16[256,1024]{1,0:T(8,128)(2,1)}, bf16[256,1024]{1,0:T(8,128)(2,1)}, u32[]{:S(2)}, u32[]{:S(2)}) collective-permute-start(bf16[256,1024]{1,0:T(8,128)(2,1)} %maximum_select_fusion.9), channel_id=1, source_target_pairs={{0,8},{4,12},{8,0},{12,4},{16,24},{20,28},{24,16},{28,20},{1,9},{5... | collective-permute-start | bytes 1572872 | tf_op jit(solution)/shard_map/ppermute | solution.py:144
  348.6 9.0 %collective-permute-done.54 = bf16[256,1024]{1,0:T(8,128)(2,1)} collective-permute-done((bf16[256,1024]{1,0:T(8,128)(2,1)}, bf16[256,1024]{1,0:T(8,128)(2,1)}, u32[]{:S(2)}, u32[]{:S(2)}) %collective-permute-start.54) | collective-permute-done | bytes 524320 | tf_op jit(solution)/shard_map/ppermute | solution.py:144
  360.6 8.2 %collective-permute-done.48 = bf16[256,1024]{1,0:T(8,128)(2,1)} collective-permute-done((bf16[256,1024]{1,0:T(8,128)(2,1)}, bf16[256,1024]{1,0:T(8,128)(2,1)}, u32[]{:S(2)}, u32[]{:S(2)}) %collective-permute-start.48) | collective-permute-done | bytes 524320 | tf_op jit(solution)/shard_map/ppermute | solution.py:144
  380.4 38.4 %attn_bwd.1 = (bf16[2176,256]{1,0:T(8,128)(2,1)}, bf16[2176,256]{1,0:T(8,128)(2,1)}, bf16[2176,256]{1,0:T(8,128)(2,1)}) custom-call(s32[3]{0:T(128)} %pad_add_fusion.bounds, bf16[2176,256]{1,0:T(8,128)(2,1)} %get-tuple-element.80.q_ref, bf16[2176,256]{1,0:T(8,128)(2,1)} %get-tuple-element.79.k_ref, bf16[2176,256]{1,0:T(8,128)(2,1)} %get-tuple-element.78.v_ref, ...), custom_call_target="tpu_custom_call" | custom-call | tf_op jit(solution)/shard_map/attn_bwd/pallas_call | solution.py:123
  422.0 3.9 fusion.90
  436.1 5.2 collective-permute-done.33
  442.2 4.2 collective-permute-done.34
  449.7 4.4 collective-permute-done.35
  454.1 9.8 %collective-permute-done.24 = bf16[512,768]{0,1:T(8,128)(2,1)S(1)} collective-permute-done((bf16[512,768]{0,1:T(8,128)(2,1)S(1)}, bf16[512,768]{0,1:T(8,128)(2,1)S(1)}, u32[]{:S(2)}, u32[]{:S(2)}) %collective-permute-start.24) | collective-permute-done | bytes 786464 | tf_op jit(solution)/shard_map/ppermute | solution.py:144
  472.7 7.7 %collective-permute-done.25 = bf16[256,768]{0,1:T(8,128)(2,1)S(1)} collective-permute-done((bf16[256,768]{0,1:T(8,128)(2,1)S(1)}, bf16[256,768]{0,1:T(8,128)(2,1)S(1)}, u32[]{:S(2)}, u32[]{:S(2)}) %collective-permute-start.25) | collective-permute-done | bytes 393248 | tf_op jit(solution)/shard_map/ppermute | solution.py:144
  480.8 3.9 collective-permute-start.26
  484.6 5.3 fusion.45
  494.6 5.2 fusion.44
  510.8 5.0 fusion.65
  539.8 4.2 collective-permute-done.42
  548.2 5.7 %collective-permute-done.43 = f32[10,1024]{1,0:T(8,128)S(1)} collective-permute-done((f32[10,1024]{1,0:T(8,128)S(1)}, f32[10,1024]{1,0:T(8,128)S(1)}, u32[]{:S(2)}, u32[]{:S(2)}) %collective-permute-start.43) | collective-permute-done | bytes 40992 | tf_op jit(solution)/shard_map/ppermute | solution.py:144
  (337 shorter events, 198.3 us)
Async XLA Ops:
  6.2 27.8 %collective-permute-start.1 = (bf16[544,1024]{1,0:T(8,128)(2,1)}, bf16[544,1024]{1,0:T(8,128)(2,1)}, u32[]{:S(2)}, u32[]{:S(2)}) collective-permute-start(bf16[544,1024]{1,0:T(8,128)(2,1)} %fusion.24), channel_id=1, source_target_pairs={{0,2},{1,3},{2,0},{3,1},{4,6},{5,7},{6,4},{7,5},{8,10},{9,11},{10,... | collective-permute-start | bytes 3342344 | tf_op jit(solution)/shard_map/ppermute | solution.py:144
  9.2 31.2 %collective-permute-start = (bf16[544,1024]{1,0:T(8,128)(2,1)}, bf16[544,1024]{1,0:T(8,128)(2,1)}, u32[]{:S(2)}, u32[]{:S(2)}) collective-permute-start(bf16[544,1024]{1,0:T(8,128)(2,1)} %fusion.24), channel_id=1, source_target_pairs={{0,1},{1,0},{2,3},{3,2},{4,5},{5,4},{6,7},{7,6},{8,9},{9,8},{10,11... | collective-permute-start | bytes 3342344 | tf_op jit(solution)/shard_map/ppermute | solution.py:144
  78.7 26.9 %collective-permute-start.5 = (bf16[544,1024]{1,0:T(8,128)(2,1)S(1)}, bf16[544,1024]{1,0:T(8,128)(2,1)S(1)}, u32[]{:S(2)}, u32[]{:S(2)}) collective-permute-start(bf16[544,1024]{1,0:T(8,128)(2,1)S(1)} %fusion.40), channel_id=1, source_target_pairs={{0,2},{1,3},{2,0},{3,1},{4,6},{5,7},{6,4},{7,5},{8,10},{9,11},{10,... | collective-permute-start | bytes 3342344 | tf_op jit(solution)/shard_map/ppermute | solution.py:144
  108.4 26.1 %collective-permute-start.7 = (bf16[544,1024]{1,0:T(8,128)(2,1)S(1)}, bf16[544,1024]{1,0:T(8,128)(2,1)S(1)}, u32[]{:S(2)}, u32[]{:S(2)}) collective-permute-start(bf16[544,1024]{1,0:T(8,128)(2,1)S(1)} %add_convert_fusion.5), channel_id=1, source_target_pairs={{0,2},{1,3},{2,0},{3,1},{4,6},{5,7},{6,4},{7,5},{8,10},{9,11},{10,... | collective-permute-start | bytes 3342344 | tf_op jit(solution)/shard_map/ppermute | solution.py:144
  110.2 24.7 %collective-permute-start.6 = (bf16[544,1024]{1,0:T(8,128)(2,1)S(1)}, bf16[544,1024]{1,0:T(8,128)(2,1)S(1)}, u32[]{:S(2)}, u32[]{:S(2)}) collective-permute-start(bf16[544,1024]{1,0:T(8,128)(2,1)S(1)} %add_convert_fusion.5), channel_id=1, source_target_pairs={{0,1},{1,0},{2,3},{3,2},{4,5},{5,4},{6,7},{7,6},{8,9},{9,8},{10,11... | collective-permute-start | bytes 3342344 | tf_op jit(solution)/shard_map/ppermute | solution.py:144
  155.5 26.7 %collective-permute-start.11 = (bf16[544,1024]{1,0:T(8,128)(2,1)S(1)}, bf16[544,1024]{1,0:T(8,128)(2,1)S(1)}, u32[]{:S(2)}, u32[]{:S(2)}) collective-permute-start(bf16[544,1024]{1,0:T(8,128)(2,1)S(1)} %fusion.36), channel_id=1, source_target_pairs={{0,2},{1,3},{2,0},{3,1},{4,6},{5,7},{6,4},{7,5},{8,10},{9,11},{10,... | collective-permute-start | bytes 3342344 | tf_op jit(solution)/shard_map/ppermute | solution.py:144
  188.3 25.9 %collective-permute-start.13 = (bf16[544,1024]{1,0:T(8,128)(2,1)S(1)}, bf16[544,1024]{1,0:T(8,128)(2,1)}, u32[]{:S(2)}, u32[]{:S(2)}) collective-permute-start(bf16[544,1024]{1,0:T(8,128)(2,1)S(1)} %get-tuple-element.38), channel_id=1, source_target_pairs={{0,2},{1,3},{2,0},{3,1},{4,6},{5,7},{6,4},{7,5},{8,10},{9,11},{10,... | collective-permute-start | bytes 3342344 | tf_op jit(solution)/shard_map/ppermute | solution.py:144
  190.0 24.1 %collective-permute-start.12 = (bf16[544,1024]{1,0:T(8,128)(2,1)S(1)}, bf16[544,1024]{1,0:T(8,128)(2,1)}, u32[]{:S(2)}, u32[]{:S(2)}) collective-permute-start(bf16[544,1024]{1,0:T(8,128)(2,1)S(1)} %get-tuple-element.38), channel_id=1, source_target_pairs={{0,1},{1,0},{2,3},{3,2},{4,5},{5,4},{6,7},{7,6},{8,9},{9,8},{10,11... | collective-permute-start | bytes 3342344 | tf_op jit(solution)/shard_map/ppermute | solution.py:144
  229.7 29.7 %collective-permute-start.50 = (bf16[512,1024]{1,0:T(8,128)(2,1)}, bf16[512,1024]{1,0:T(8,128)(2,1)}, u32[]{:S(2)}, u32[]{:S(2)}) collective-permute-start(bf16[512,1024]{1,0:T(8,128)(2,1)} %dynamic-slice_convert_fusion), channel_id=1, source_target_pairs={{0,4},{4,0},{8,12},{12,8},{16,20},{20,16},{24,28},{28,24},{1,5},{5... | collective-permute-start | bytes 3145736 | tf_op jit(solution)/shard_map/ppermute | solution.py:144
  255.8 25.9 %collective-permute-start.44 = (bf16[512,1024]{1,0:T(8,128)(2,1)}, bf16[512,1024]{1,0:T(8,128)(2,1)}, u32[]{:S(2)}, u32[]{:S(2)}) collective-permute-start(bf16[512,1024]{1,0:T(8,128)(2,1)} %dynamic-slice_convert_fusion.1), channel_id=1, source_target_pairs={{0,4},{4,0},{8,12},{12,8},{16,20},{20,16},{24,28},{28,24},{1,5},{5... | collective-permute-start | bytes 3145736 | tf_op jit(solution)/shard_map/ppermute | solution.py:144
  256.0 29.7 %collective-permute-start.15 = (bf16[544,1024]{1,0:T(8,128)(2,1)S(1)}, bf16[544,1024]{1,0:T(8,128)(2,1)S(1)}, u32[]{:S(2)}, u32[]{:S(2)}) collective-permute-start(bf16[544,1024]{1,0:T(8,128)(2,1)S(1)} %get-tuple-element.64), channel_id=1, source_target_pairs={{0,1},{1,0},{2,3},{3,2},{4,5},{5,4},{6,7},{7,6},{8,9},{9,8},{10,11... | collective-permute-start | bytes 3342344 | tf_op jit(solution)/shard_map/ppermute | solution.py:144
  257.7 28.1 %collective-permute-start.17 = (bf16[544,1024]{1,0:T(8,128)(2,1)}, bf16[544,1024]{1,0:T(8,128)(2,1)S(1)}, u32[]{:S(2)}, u32[]{:S(2)}) collective-permute-start(bf16[544,1024]{1,0:T(8,128)(2,1)} %fusion.34), channel_id=1, source_target_pairs={{0,2},{1,3},{2,0},{3,1},{4,6},{5,7},{6,4},{7,5},{8,10},{9,11},{10,... | collective-permute-start | bytes 3342344 | tf_op jit(solution)/shard_map/ppermute | solution.py:144
  262.7 33.1 %collective-permute-start.51 = (bf16[256,1024]{1,0:T(8,128)(2,1)}, bf16[256,1024]{1,0:T(8,128)(2,1)}, u32[]{:S(2)}, u32[]{:S(2)}) collective-permute-start(bf16[256,1024]{1,0:T(8,128)(2,1)} %dynamic-slice_convert_fusion.3), channel_id=1, source_target_pairs={{0,8},{4,12},{8,0},{12,4},{16,24},{20,28},{24,16},{28,20},{1,9},{5... | collective-permute-start | bytes 1572872 | tf_op jit(solution)/shard_map/ppermute | solution.py:144
  284.1 16.9 %collective-permute-start.45 = (bf16[256,1024]{1,0:T(8,128)(2,1)}, bf16[256,1024]{1,0:T(8,128)(2,1)}, u32[]{:S(2)}, u32[]{:S(2)}) collective-permute-start(bf16[256,1024]{1,0:T(8,128)(2,1)} %dynamic-slice_convert_fusion.4), channel_id=1, source_target_pairs={{0,8},{4,12},{8,0},{12,4},{16,24},{20,28},{24,16},{28,20},{1,9},{5... | collective-permute-start | bytes 1572872 | tf_op jit(solution)/shard_map/ppermute | solution.py:144
  294.4 26.1 %collective-permute-start.19 = (bf16[544,1024]{1,0:T(8,128)(2,1)S(1)}, bf16[544,1024]{1,0:T(8,128)(2,1)}, u32[]{:S(2)}, u32[]{:S(2)}) collective-permute-start(bf16[544,1024]{1,0:T(8,128)(2,1)S(1)} %get-tuple-element.40), channel_id=1, source_target_pairs={{0,2},{1,3},{2,0},{3,1},{4,6},{5,7},{6,4},{7,5},{8,10},{9,11},{10,... | collective-permute-start | bytes 3342344 | tf_op jit(solution)/shard_map/ppermute | solution.py:144
  298.4 20.2 %collective-permute-start.52 = (bf16[128,1024]{1,0:T(8,128)(2,1)}, bf16[128,1024]{1,0:T(8,128)(2,1)}, u32[]{:S(2)}, u32[]{:S(2)}) collective-permute-start(bf16[128,1024]{1,0:T(8,128)(2,1)} %dynamic-slice_convert_fusion.6), channel_id=1, source_target_pairs={{0,16},{4,20},{8,24},{12,28},{16,0},{20,4},{24,8},{28,12},{1,17},{... | collective-permute-start | bytes 786440 | tf_op jit(solution)/shard_map/ppermute | solution.py:144
  304.9 24.8 %collective-permute-start.46 = (bf16[128,1024]{1,0:T(8,128)(2,1)}, bf16[128,1024]{1,0:T(8,128)(2,1)}, u32[]{:S(2)}, u32[]{:S(2)}) collective-permute-start(bf16[128,1024]{1,0:T(8,128)(2,1)} %dynamic-slice_convert_fusion.7), channel_id=1, source_target_pairs={{0,16},{4,20},{8,24},{12,28},{16,0},{20,4},{24,8},{28,12},{1,17},{... | collective-permute-start | bytes 786440 | tf_op jit(solution)/shard_map/ppermute | solution.py:144
  320.5 14.8 %collective-permute-start.53 = (bf16[128,1024]{1,0:T(8,128)(2,1)}, bf16[128,1024]{1,0:T(8,128)(2,1)}, u32[]{:S(2)}, u32[]{:S(2)}) collective-permute-start(bf16[128,1024]{1,0:T(8,128)(2,1)} %add_convert_fusion.6), channel_id=1, source_target_pairs={{0,16},{4,20},{8,24},{12,28},{16,0},{20,4},{24,8},{28,12},{1,17},{... | collective-permute-start | bytes 786440 | tf_op jit(solution)/shard_map/ppermute | solution.py:144
  320.5 51.4 %collective-permute-start.18 = (bf16[544,1024]{1,0:T(8,128)(2,1)S(1)}, bf16[544,1024]{1,0:T(8,128)(2,1)}, u32[]{:S(2)}, u32[]{:S(2)}) collective-permute-start(bf16[544,1024]{1,0:T(8,128)(2,1)S(1)} %get-tuple-element.40), channel_id=1, source_target_pairs={{0,1},{1,0},{2,3},{3,2},{4,5},{5,4},{6,7},{7,6},{8,9},{9,8},{10,11... | collective-permute-start | bytes 3342344 | tf_op jit(solution)/shard_map/ppermute | solution.py:144
  320.5 51.4 %collective-permute-start.20 = (bf16[544,1024]{1,0:T(8,128)(2,1)}, bf16[544,1024]{1,0:T(8,128)(2,1)}, u32[]{:S(2)}, u32[]{:S(2)}) collective-permute-start(bf16[544,1024]{1,0:T(8,128)(2,1)} %collective-permute-done.19), channel_id=1, source_target_pairs={{0,1},{1,0},{2,3},{3,2},{4,5},{5,4},{6,7},{7,6},{8,9},{9,8},{10,11... | collective-permute-start | bytes 3342344 | tf_op jit(solution)/shard_map/ppermute | solution.py:144
  331.6 14.8 %collective-permute-start.47 = (bf16[128,1024]{1,0:T(8,128)(2,1)}, bf16[128,1024]{1,0:T(8,128)(2,1)}, u32[]{:S(2)}, u32[]{:S(2)}) collective-permute-start(bf16[128,1024]{1,0:T(8,128)(2,1)} %add_convert_fusion.7), channel_id=1, source_target_pairs={{0,16},{4,20},{8,24},{12,28},{16,0},{20,4},{24,8},{28,12},{1,17},{... | collective-permute-start | bytes 786440 | tf_op jit(solution)/shard_map/ppermute | solution.py:144
  337.5 20.1 %collective-permute-start.54 = (bf16[256,1024]{1,0:T(8,128)(2,1)}, bf16[256,1024]{1,0:T(8,128)(2,1)}, u32[]{:S(2)}, u32[]{:S(2)}) collective-permute-start(bf16[256,1024]{1,0:T(8,128)(2,1)} %maximum_select_fusion.9), channel_id=1, source_target_pairs={{0,8},{4,12},{8,0},{12,4},{16,24},{20,28},{24,16},{28,20},{1,9},{5... | collective-permute-start | bytes 1572872 | tf_op jit(solution)/shard_map/ppermute | solution.py:144
  348.6 20.2 %collective-permute-start.48 = (bf16[256,1024]{1,0:T(8,128)(2,1)}, bf16[256,1024]{1,0:T(8,128)(2,1)}, u32[]{:S(2)}, u32[]{:S(2)}) collective-permute-start(bf16[256,1024]{1,0:T(8,128)(2,1)} %maximum_select_fusion.8), channel_id=1, source_target_pairs={{0,8},{4,12},{8,0},{12,4},{16,24},{20,28},{24,16},{28,20},{1,9},{5... | collective-permute-start | bytes 1572872 | tf_op jit(solution)/shard_map/ppermute | solution.py:144
  360.6 120.1 %collective-permute-start.55 = (bf16[512,1024]{1,0:T(8,128)(2,1)}, bf16[512,1024]{1,0:T(8,128)(2,1)}, u32[]{:S(2)}, u32[]{:S(2)}) collective-permute-start(bf16[512,1024]{1,0:T(8,128)(2,1)} %maximum_select_fusion.4), channel_id=1, source_target_pairs={{0,4},{4,0},{8,12},{12,8},{16,20},{20,16},{24,28},{28,24},{1,5},{5... | collective-permute-start | bytes 3145736 | tf_op jit(solution)/shard_map/ppermute | solution.py:144
  371.9 122.4 %collective-permute-start.49 = (bf16[512,1024]{1,0:T(8,128)(2,1)}, bf16[512,1024]{1,0:T(8,128)(2,1)}, u32[]{:S(2)}, u32[]{:S(2)}) collective-permute-start(bf16[512,1024]{1,0:T(8,128)(2,1)} %maximum_select_fusion.3), channel_id=1, source_target_pairs={{0,4},{4,0},{8,12},{12,8},{16,20},{20,16},{24,28},{28,24},{1,5},{5... | collective-permute-start | bytes 3145736 | tf_op jit(solution)/shard_map/ppermute | solution.py:144
  432.2 38.3 %collective-permute-start.22 = (bf16[544,1024]{1,0:T(8,128)(2,1)S(1)}, bf16[544,1024]{1,0:T(8,128)(2,1)S(1)}, u32[]{:S(2)}, u32[]{:S(2)}) collective-permute-start(bf16[544,1024]{1,0:T(8,128)(2,1)S(1)} %get-tuple-element.59), channel_id=1, source_target_pairs={{0,1},{1,0},{2,3},{3,2},{4,5},{5,4},{6,7},{7,6},{8,9},{9,8},{10,11... | collective-permute-start | bytes 3342344 | tf_op jit(solution)/shard_map/ppermute | solution.py:144
  435.1 13.1 %collective-permute-start.30 = (f32[1536]{0:T(1024)S(1)}, f32[1536]{0:T(1024)S(1)}, u32[]{:S(2)}, u32[]{:S(2)}) collective-permute-start(f32[1536]{0:T(1024)S(1)} %pad_maximum_fusion.6), channel_id=1, source_target_pairs={{0,16},{4,20},{8,24},{12,28},{16,0},{20,4},{24,8},{28,12},{1,17},{... | collective-permute-start | bytes 18440 | tf_op jit(solution)/shard_map/ppermute | solution.py:144
  446.4 17.5 %collective-permute-start.24 = (bf16[512,768]{0,1:T(8,128)(2,1)S(1)}, bf16[512,768]{0,1:T(8,128)(2,1)S(1)}, u32[]{:S(2)}, u32[]{:S(2)}) collective-permute-start(bf16[512,768]{0,1:T(8,128)(2,1)S(1)} %dynamic-slice_convert_fusion.2), channel_id=1, source_target_pairs={{0,4},{4,0},{8,12},{12,8},{16,20},{20,16},{24,28},{28,24},{1,5},{5... | collective-permute-start | bytes 2359304 | tf_op jit(solution)/shard_map/ppermute | solution.py:144
  454.1 56.7 %collective-permute-start.21 = (bf16[544,1024]{1,0:T(8,128)(2,1)}, bf16[544,1024]{1,0:T(8,128)(2,1)}, u32[]{:S(2)}, u32[]{:S(2)}) collective-permute-start(bf16[544,1024]{1,0:T(8,128)(2,1)} %get-tuple-element.58), channel_id=1, source_target_pairs={{0,1},{1,0},{2,3},{3,2},{4,5},{5,4},{6,7},{7,6},{8,9},{9,8},{10,11... | collective-permute-start | bytes 3342344 | tf_op jit(solution)/shard_map/ppermute | solution.py:144
  480.5 30.3 %collective-permute-start.23 = (bf16[544,1024]{1,0:T(8,128)(2,1)}, bf16[544,1024]{1,0:T(8,128)(2,1)}, u32[]{:S(2)}, u32[]{:S(2)}) collective-permute-start(bf16[544,1024]{1,0:T(8,128)(2,1)} %fusion.31), channel_id=1, source_target_pairs={{0,2},{1,3},{2,0},{3,1},{4,6},{5,7},{6,4},{7,5},{8,10},{9,11},{10,... | collective-permute-start | bytes 3342344 | tf_op jit(solution)/shard_map/ppermute | solution.py:144
  507.8 20.1 %collective-permute-start.28 = (bf16[256,768]{0,1:T(8,128)(2,1)}, bf16[256,768]{0,1:T(8,128)(2,1)}, u32[]{:S(2)}, u32[]{:S(2)}) collective-permute-start(bf16[256,768]{0,1:T(8,128)(2,1)} %maximum_select_fusion.11), channel_id=1, source_target_pairs={{0,8},{4,12},{8,0},{12,4},{16,24},{20,28},{24,16},{28,20},{1,9},{5... | collective-permute-start | bytes 1179656 | tf_op jit(solution)/shard_map/ppermute | solution.py:144
  532.3 22.8 %collective-permute-start.29 = (bf16[512,768]{0,1:T(8,128)(2,1)}, bf16[512,768]{0,1:T(8,128)(2,1)}, u32[]{:S(2)}, u32[]{:S(2)}) collective-permute-start(bf16[512,768]{0,1:T(8,128)(2,1)} %maximum_select_fusion.6), channel_id=1, source_target_pairs={{0,4},{4,0},{8,12},{12,8},{16,20},{20,16},{24,28},{28,24},{1,5},{5... | collective-permute-start | bytes 2359304 | tf_op jit(solution)/shard_map/ppermute | solution.py:144
  (78 other events, 990.4 us)

commit v2 on v1

--- a/solution.py
+++ b/solution.py
@@ -6,6 +6,7 @@
 from jax.sharding import PartitionSpec as P
 HEAD=64; IMG=1024; CAP_MIN=5; LANES=128
 F32=jnp.float32; BF=jnp.bfloat16
+MESH=pl.DeviceIdType.MESH
 NT=(((1,),(1,)),((),()))
 TN=(((0,),(0,)),((),()))
 
@@ -196,6 +197,424 @@
     return values
 
 
+SLOT = {1: 0, 3: 1, 2: 2, 0: 3}
+TILE = 256
+
+
+def spans_of(rows):
+    units = rows // 16
+    sizes = [16 * (units // 4 + (1 if i < units % 4 else 0)) for i in range(4)]
+    edges = [sum(sizes[:i]) for i in range(5)]
+    return [(edges[i], edges[i + 1]) for i in range(4)]
+
+
+def fold8(values):
+    rows, cols = values.shape
+    return jnp.sum(values.reshape(rows // 8, 8, cols), axis=0)
+
+
+def norm_stats(values):
+    center = values - jnp.mean(values, axis=-1, keepdims=True)
+    inv = lax.rsqrt(jnp.mean(center * center, axis=-1, keepdims=True) + eps_norm)
+    return center * inv, inv
+
+
+def norm_pull(upstream, gain, unit, inv):
+    scaled = upstream * gain
+    first = jnp.mean(scaled, axis=-1, keepdims=True)
+    second = jnp.mean(scaled * unit, axis=-1, keepdims=True)
+    return (scaled - first - unit * second) * inv
+
+
+def mid_kernel(
+    heads, tokens, cot, wout, w1, w2, b1, vec,
+    mixed, ghid, ghead, w2g, w1g, wog, sums, b1sum,
+    hs, mlp, act, dgel, brn, gpre, u1, u2, hid, r1, r2, pbuf, cs, cr, xs, xr, acc, b1acc, stage,
+    send, recv, local_sem,
+):
+    local, width = tokens.shape
+    hidden_units = w1.shape[1]
+    spans = spans_of(local)
+    count = len(spans)
+    dp, me = lax.axis_index("dp"), lax.axis_index("mp")
+    mx, mc = me // 2, me % 2
+    peer_core = (dp, mx * 2 + 1 - mc)
+    peer_x = (dp, (1 - mx) * 2 + mc)
+    owner = {0: me, 1: mx * 2 + 1 - mc, 2: (1 - mx) * 2 + mc, 3: (1 - mx) * 2 + 1 - mc}
+
+    barrier = pltpu.get_barrier_semaphore()
+    for peer in (peer_core, peer_x):
+        pl.semaphore_signal(barrier, inc=1, device_id=peer, device_id_type=MESH)
+    pl.semaphore_wait(barrier, 2)
+
+    def remote(src, dst, phase, kind, c, device):
+        i = (phase * 5 + kind) * count + c
+        return pltpu.make_async_remote_copy(
+            src_ref=src, dst_ref=dst, send_sem=send.at[i], recv_sem=recv.at[i], device_id=device, device_id_type=MESH
+        )
+
+    def core_copy(phase, c):
+        lo, hi = spans[c]
+        rows = pl.ds(2 * lo, 2 * (hi - lo))
+        return remote(cs.at[rows], cr.at[rows], phase, 0, c, peer_core)
+
+    def x_copy(phase, c):
+        lo, hi = spans[c]
+        rows = pl.ds(lo, hi - lo)
+        return remote(xs.at[rows], xr.at[rows], phase, 1, c, peer_x)
+
+    def block(c, j):
+        lo, hi = spans[c]
+        return pl.ds(4 * lo + SLOT[j] * (hi - lo), hi - lo)
+
+    def gather_copies(full, phase, c):
+        own = full.at[block(c, 0)]
+        return (
+            remote(own, full.at[block(c, 2)], phase, 2, c, peer_x),
+            remote(own, full.at[block(c, 1)], phase, 3, c, peer_core),
+            remote(full.at[block(c, 2)], full.at[block(c, 3)], phase, 4, c, peer_core),
+        )
+
+    def tiles(c):
+        lo, hi = spans[c]
+        step = next(t for t in (48, 64, 32, 16) if (hi - lo) % t == 0)
+        return (hi - lo) // step, step
+
+    def start_gather(full, phase, c):
+        first, second, _ = gather_copies(full, phase, c)
+        first.start()
+        second.start()
+
+    def forward(full, phase, c):
+        first, second, third = gather_copies(full, phase, c)
+        first.wait_recv()
+        third.start()
+        second.wait_recv()
+        third.wait_recv()
+
+    def partial_products(lhs, rhs, turned, phase, c, half, wide=TILE):
+        lo, hi = spans[c]
+        r = hi - lo
+        rows = pl.ds(4 * lo + half * 2 * r, 2 * r)
+        out = pl.ds(2 * lo, 2 * r)
+
+        def body(n, carry):
+            cols = pl.ds(pl.multiple_of(n * wide, wide), wide)
+            if turned:
+                part = lax.dot_general(lhs[rows, :], rhs[cols, :], NT, preferred_element_type=F32)
+            else:
+                part = jnp.dot(lhs[rows, :], rhs[:, cols], preferred_element_type=F32)
+            if half == 0:
+                cs[out, cols] = part.astype(BF)
+            else:
+                pbuf[out, cols] = part
+            return carry
+
+        lax.fori_loop(0, width // wide, body, 0)
+
+    def pass_on(phase, c):
+        lo, hi = spans[c]
+        r = hi - lo
+        core_copy(phase, c).wait_recv()
+        if phase:
+            x_copy(phase - 1, c).wait_send()
+        xs[lo:hi, :] = (pbuf[2 * lo:2 * lo + r, :] + cr[2 * lo + r:2 * lo + 2 * r, :].astype(F32)).astype(BF)
+        x_copy(phase, c).start()
+
+    def own_total(c, i, step):
+        lo, hi = spans[c]
+        r = hi - lo
+        kept = pl.ds(pl.multiple_of(2 * lo + r + i * step, 16), step)
+        near = pl.ds(pl.multiple_of(2 * lo + i * step, 16), step)
+        far = pl.ds(pl.multiple_of(lo + i * step, 16), step)
+        return far, pbuf[kept, :] + cr[near, :].astype(F32) + xr[far, :].astype(F32)
+
+    def row(i):
+        return vec[i:i + 1, :]
+
+    acc[...] = jnp.zeros_like(acc)
+    b1acc[...] = jnp.zeros_like(b1acc)
+
+    def add(i, values):
+        acc[8 * i:8 * i + 8, :] += fold8(values)
+
+    def project(c):
+        lo, hi = spans[c]
+        for j in (1, 3, 2, 0):
+            start = pl.multiple_of(owner[j] * local + lo, 16)
+            hs[block(c, j), :] = heads[pl.ds(start, hi - lo), :]
+        partial_products(hs, wout, False, 0, c, 0)
+        core_copy(0, c).start()
+        partial_products(hs, wout, False, 0, c, 1)
+
+    project(0)
+    for c in range(count):
+        if c + 1 < count:
+            project(c + 1)
+        pass_on(0, c)
+
+    for c in range(count):
+        x_copy(0, c).wait_recv()
+        lo, hi = spans[c]
+        trips, step = tiles(c)
+
+        def norms(i, carry):
+            rows, total = own_total(c, i, step)
+            unit, inv = norm_stats(total + row(0))
+            u1[rows, :] = unit
+            r1[rows, :] = jnp.broadcast_to(inv, (step, LANES))
+            hidden = tokens[rows, :].astype(F32) + unit * row(2) + row(3)
+            hid[rows, :] = hidden
+            unit, inv = norm_stats(hidden)
+            u2[rows, :] = unit
+            r2[rows, :] = jnp.broadcast_to(inv, (step, LANES))
+            dst = pl.ds(pl.multiple_of(4 * lo + SLOT[0] * (hi - lo) + i * step, 16), step)
+            mlp[dst, :] = (unit * row(4) + row(5)).astype(BF)
+            return carry
+
+        lax.fori_loop(0, trips, norms, 0)
+        start_gather(mlp, 0, c)
+
+    for c in range(count):
+        lo, hi = spans[c]
+        r = hi - lo
+        forward(mlp, 0, c)
+        core_copy(0, c).wait_send()
+        for half in range(2):
+            rows = pl.ds(4 * lo + half * 2 * r, 2 * r)
+
+            def units(n, carry):
+                cols = pl.ds(pl.multiple_of(n * TILE, TILE), TILE)
+                pre = jnp.dot(mlp[rows, :], w1[:, cols], preferred_element_type=F32) + b1[:, cols]
+                square = pre * pre
+                inner = (0.7978845608028654 * pre) * (1.0 + 0.044715 * square)
+                tanh = jnp.tanh(inner)
+                plus = 0.5 * (1.0 + tanh)
+                act[rows, cols] = (pre * plus).astype(BF)
+                slope = plus + (0.5 * pre) * (1.0 - tanh * tanh) * (
+                    0.7978845608028654 * (1.0 + (3 * 0.044715) * square)
+                )
+                dgel[rows, cols] = slope.astype(BF)
+                return carry
+
+            lax.fori_loop(0, hidden_units // TILE, units, 0)
+            partial_products(act, w2, False, 1, c, half)
+            if half == 0:
+                core_copy(1, c).start()
+        pass_on(1, c)
+
+    for c in range(count):
+        x_copy(1, c).wait_recv()
+        lo, hi = spans[c]
+        trips, step = tiles(c)
+
+        def last(i, carry):
+            rows, total = own_total(c, i, step)
+            unit, inv = norm_stats(total + row(1))
+            mixed[rows, :] = (hid[rows, :] + unit * row(6) + row(7)).astype(BF)
+            grad = cot[rows, :].astype(F32)
+            add(2, grad * unit)
+            add(5, grad)
+            low = norm_pull(grad, row(6), unit, inv).astype(BF)
+            add(7, low.astype(F32))
+            dst = pl.ds(pl.multiple_of(4 * lo + SLOT[0] * (hi - lo) + i * step, 16), step)
+            brn[dst, :] = low
+            return carry
+
+        lax.fori_loop(0, trips, last, 0)
+        start_gather(brn, 1, c)
+
+    for c in range(count):
+        lo, hi = spans[c]
+        r = hi - lo
+        forward(brn, 1, c)
+        core_copy(1, c).wait_send()
+        for half in range(2):
+            rows = pl.ds(4 * lo + half * 2 * r, 2 * r)
+
+            def slopes(n, carry):
+                cols = pl.ds(pl.multiple_of(n * TILE, TILE), TILE)
+                grad = lax.dot_general(brn[rows, :], w2[cols, :], NT, preferred_element_type=F32)
+                low = (grad * dgel[rows, cols].astype(F32)).astype(BF)
+                gpre[rows, cols] = low
+                b1acc[:, cols] += fold8(low.astype(F32))
+                return carry
+
+            lax.fori_loop(0, hidden_units // TILE, slopes, 0)
+            partial_products(gpre, w1, True, 2, c, half)
+            if half == 0:
+                core_copy(2, c).start()
+        pass_on(2, c)
+
+    def weight_grad(lhs, rhs, dst, first_slot):
+        trips = lhs.shape[1] // TILE
+
+        def out(n, slot):
+            return pltpu.make_async_copy(
+                stage.at[slot], dst.at[pl.ds(n * TILE, TILE)], local_sem.at[first_slot + n]
+            )
+
+        for n in range(trips):
+            if n >= 2:
+                out(n - 2, n % 2).wait()
+            stage[n % 2] = lax.dot_general(
+                lhs[:, n * TILE:(n + 1) * TILE], rhs[...], TN, preferred_element_type=F32
+            )
+            out(n, n % 2).start()
+        for n in range(max(0, trips - 2), trips):
+            out(n, n % 2).wait()
+
+    weight_grad(act, brn, w2g, 0)
+
+    for c in range(count):
+        x_copy(2, c).wait_recv()
+        lo, hi = spans[c]
+        trips, step = tiles(c)
+
+        def pulls(i, carry):
+            rows, total = own_total(c, i, step)
+            unit = u2[rows, :]
+            add(1, total * unit)
+            add(4, total)
+            grad = cot[rows, :].astype(F32) + norm_pull(total, row(4), unit, r2[rows, 0:1])
+            ghid[rows, :] = grad
+            unit = u1[rows, :]
+            add(0, grad * unit)
+            add(3, grad)
+            low = norm_pull(grad, row(2), unit, r1[rows, 0:1]).astype(BF)
+            add(6, low.astype(F32))
+            dst = pl.ds(pl.multiple_of(4 * lo + SLOT[0] * (hi - lo) + i * step, 16), step)
+            dgel[dst, :] = low
+            return carry
+
+        lax.fori_loop(0, trips, pulls, 0)
+        start_gather(dgel, 2, c)
+
+    weight_grad(mlp, gpre, w1g, width // TILE)
+
+    for c in range(count):
+        lo, hi = spans[c]
+        forward(dgel, 2, c)
+        for j in (1, 3, 2, 0):
+            start = pl.multiple_of(owner[j] * local + lo, 16)
+            ghead[pl.ds(start, hi - lo), :] = lax.dot_general(
+                dgel[block(c, j), :], wout[...], NT, preferred_element_type=F32
+            ).astype(BF)
+    weight_grad(hs, dgel, wog, 2 * (width // TILE))
+
+    for i in range(8):
+        sums[i:i + 1, :] = jnp.sum(acc[8 * i:8 * i + 8, :], axis=0, keepdims=True)
+    b1sum[...] = jnp.sum(b1acc[...], axis=0, keepdims=True)
+
+    for c in range(count):
+        core_copy(2, c).wait_send()
+        x_copy(2, c).wait_send()
+        for phase, full in ((0, mlp), (1, brn), (2, dgel)):
+            for copy in gather_copies(full, phase, c):
+                copy.wait_send()
+
+
+def middle(heads, tokens, cot, wout, w1, w2, b1, vec):
+    seq, part = heads.shape
+    local, width = tokens.shape
+    units = w1.shape[1]
+    vmem = pl.BlockSpec(memory_space=pltpu.VMEM)
+    any_spec = pl.BlockSpec(memory_space=pl.ANY)
+    shape = jax.ShapeDtypeStruct
+    copies = 15 * 4
+    return pl.pallas_call(
+        mid_kernel,
+        in_specs=[vmem] * 8,
+        out_specs=[vmem, vmem, vmem, any_spec, any_spec, any_spec, vmem, vmem],
+        out_shape=[
+            shape((local, width), BF), shape((local, width), F32), shape((seq, part), BF),
+            shape((units, width), F32), shape((width, units), F32), shape((part, width), F32),
+            shape((8, width), F32), shape((1, units), F32),
+        ],
+        scratch_shapes=[
+            pltpu.VMEM((seq, part), BF), pltpu.VMEM((seq, width), BF), pltpu.VMEM((seq, units), BF),
+            pltpu.VMEM((seq, units), BF), pltpu.VMEM((seq, width), BF), pltpu.VMEM((seq, units), BF),
+            pltpu.VMEM((local, width), F32), pltpu.VMEM((local, width), F32), pltpu.VMEM((local, width), F32),
+            pltpu.VMEM((local, LANES), F32), pltpu.VMEM((local, LANES), F32),
+            pltpu.VMEM((2 * local, width), F32), pltpu.VMEM((2 * local, width), BF),
+            pltpu.VMEM((2 * local, width), BF), pltpu.VMEM((local, width), BF), pltpu.VMEM((local, width), BF),
+            pltpu.VMEM((64, width), F32), pltpu.VMEM((8, units), F32), pltpu.VMEM((2, TILE, width), F32),
+            pltpu.SemaphoreType.DMA((copies,)), pltpu.SemaphoreType.DMA((copies,)), pltpu.SemaphoreType.DMA((16,)),
+        ],
+        compiler_params=pltpu.CompilerParams(collective_id=0, has_side_effects=True, vmem_limit_bytes=63 << 20),
+        cost_estimate=pl.CostEstimate(
+            flops=14 * seq * width * units, bytes_accessed=40 << 20, transcendentals=seq * units
+        ),
+        name="middle",
+    )(heads, tokens, cot, wout, w1, w2, b1, vec)
+
+
+def middle_by_ops(head_low, rows_in, cotangent, wout, out_bias, w1, b1, w2, b2, gains, shifts, rel_of, sort):
+    local_rows, width = rows_in.shape
+    size = lax.axis_size("mp")
+    seq_len, head_part = head_low.shape
+    head_rel = rel_of(head_low)
+    grad_out_all = cotangent.astype(F32)
+    state = []
+    for lo, hi in [(0, local_rows)]:
+        rows = hi - lo
+        total = size * rows
+        attn_out = scatter_rel(
+            jnp.dot(head_rel[:, lo:hi], wout, preferred_element_type=F32), "mp"
+        ) + out_bias.astype(F32)
+        norm_b, pull_b = jax.vjp(layer_norm, attn_out, gains[1], shifts[1])
+        hidden_rows = rows_in[lo:hi] + norm_b
+        norm_c, pull_c = jax.vjp(layer_norm, hidden_rows, gains[2], shifts[2])
+        mlp_full = gather_rel(norm_c.astype(BF), "mp").reshape(total, width)
+        pre_act = jnp.dot(mlp_full, w1, preferred_element_type=F32) + b1.astype(F32)
+        activated, gelu_pull = jax.vjp(gelu_tanh, pre_act)
+        act_low = activated.astype(BF)
+        branch = scatter_rel(
+            jnp.dot(act_low, w2, preferred_element_type=F32).reshape(size, rows, width), "mp"
+        ) + b2.astype(F32)
+        norm_d, pull_d = jax.vjp(layer_norm, branch, gains[3], shifts[3])
+        mixed = (hidden_rows + norm_d).astype(BF)
+        grad_out = grad_out_all[lo:hi]
+        grad_branch, gain_d, shift_d = pull_d(grad_out)
+        branch_low = grad_branch.astype(BF)
+        b2_part = jnp.sum(branch_low.astype(F32), axis=0)
+        branch_full = gather_rel(branch_low, "mp").reshape(total, width)
+        grad_act = jnp.einsum("td,fd->tf", branch_full, w2, preferred_element_type=F32)
+        grad_pre = gelu_pull(grad_act)[0].astype(BF)
+        b1_part = jnp.sum(grad_pre.astype(F32), axis=0)
+        grad_norm_c = scatter_rel(
+            jnp.einsum("tf,df->td", grad_pre, w1, preferred_element_type=F32).reshape(size, rows, width), "mp"
+        )
+        grad_hidden_c, gain_c, shift_c = pull_c(grad_norm_c)
+        grad_hidden = grad_out + grad_hidden_c
+        grad_attn, gain_b, shift_b = pull_b(grad_hidden)
+        attn_grad_low = grad_attn.astype(BF)
+        out_bias_part = jnp.sum(attn_grad_low.astype(F32), axis=0)
+        attn_grad_rel = gather_rel(attn_grad_low, "mp")
+        state.append(dict(
+            mixed=mixed, act=act_low, branch=branch_full, mlp=mlp_full, pre=grad_pre, hidden=grad_hidden,
+            attn=attn_grad_rel, heads=head_rel[:, lo:hi].reshape(total, head_part),
+            gh=jnp.einsum("jtd,cd->jtc", attn_grad_rel, wout, preferred_element_type=F32).astype(BF),
+            sums=jnp.stack([gain_b, gain_c, gain_d, shift_b, shift_c, shift_d, out_bias_part, b2_part]),
+            b1=b1_part,
+        ))
+
+    def joined(name, axis=0):
+        return jnp.concatenate([s[name] for s in state], axis=axis)
+
+    w2_grad = jnp.einsum("tf,td->fd", joined("act"), joined("branch"), preferred_element_type=F32)
+    w1_grad = jnp.einsum("td,tf->df", joined("mlp"), joined("pre"), preferred_element_type=F32)
+    attn_grad_full = joined("attn", 1).reshape(seq_len, width)
+    wout_grad = jnp.einsum(
+        "tc,td->cd", head_rel.reshape(seq_len, head_part), attn_grad_full, preferred_element_type=F32
+    )
+    grad_heads = sort(joined("gh", 1))
+    mixed, grad_hidden = joined("mixed"), joined("hidden")
+    mid_sums = sum(s["sums"] for s in state)
+    b1_grad = sum(s["b1"] for s in state)
+    return mixed, grad_hidden, grad_heads, w2_grad, w1_grad, wout_grad, mid_sums, b1_grad
+
+
 def shards(
     tokens, caption_len, row_offset, wqkv, qv_bias, wout, out_bias, w1, b1, w2, b2, ln_gain, ln_bias, cotangent,
 ):
@@ -232,45 +651,21 @@
     projected = (projected + bias3).astype(BF)
     queries, keys, values = [projected[:, i * head_part:(i + 1) * head_part] for i in range(3)]
     head_low, lse = attn_fwd(bounds, queries, keys, values)
-    head_rel = rel_of(head_low)
-    attn_out = scatter_rel(jnp.dot(head_rel, wout, preferred_element_type=F32), "mp") + out_bias.astype(F32)
-    norm_b, pull_b = jax.vjp(layer_norm, attn_out, gains[1], shifts[1])
-    hidden_rows = rows_in + norm_b
-    norm_c, pull_c = jax.vjp(layer_norm, hidden_rows, gains[2], shifts[2])
-    mlp_rel = gather_rel(norm_c.astype(BF), "mp")
-    mlp_full = mlp_rel.reshape(seq_len, width)
-    pre_act = jnp.dot(mlp_full, w1, preferred_element_type=F32) + b1.astype(F32)
-    activated, gelu_pull = jax.vjp(gelu_tanh, pre_act)
-    act_low = activated.astype(BF)
-    branch = scatter_rel(
-        jnp.dot(act_low, w2, preferred_element_type=F32).reshape(size, local_rows, width), "mp"
-    ) + b2.astype(F32)
-    norm_d, pull_d = jax.vjp(layer_norm, branch, gains[3], shifts[3])
-    mixed = (hidden_rows + norm_d).astype(BF)
-    grad_out = cotangent.astype(F32)
-    grad_branch, gain_d, shift_d = pull_d(grad_out)
-    branch_low = grad_branch.astype(BF)
-    b2_part = jnp.sum(branch_low.astype(F32), axis=0)
-    branch_full = gather_rel(branch_low, "mp").reshape(seq_len, width)
-    w2_grad = jnp.einsum("tf,td->fd", act_low, branch_full, preferred_element_type=F32)
+    if size == 4 and local_rows % 16 == 0 and w1.shape[1] % TILE == 0 and head_part % TILE == 0:
+        vec = jnp.stack(
+            [out_bias.astype(F32), b2.astype(F32), gains[1], shifts[1], gains[2], shifts[2], gains[3], shifts[3]]
+        )
+        mixed, grad_hidden, grad_heads, w2_grad, w1_grad, wout_grad, mid_sums, b1_grad = middle(
+            head_low, tokens, cotangent, wout, w1, w2, b1.astype(F32)[None], vec
+        )
+        b1_grad = b1_grad[0]
+    else:
+        mixed, grad_hidden, grad_heads, w2_grad, w1_grad, wout_grad, mid_sums, b1_grad = middle_by_ops(
+            head_low, rows_in, cotangent, wout, out_bias, w1, b1, w2, b2, gains, shifts, rel_of, sort
+        )
     w2_grad = reduce_all(w2_grad, "dp")
-    grad_act = jnp.einsum("td,fd->tf", branch_full, w2, preferred_element_type=F32)
-    grad_pre = gelu_pull(grad_act)[0].astype(BF)
-    b1_grad = jnp.sum(grad_pre.astype(F32), axis=0)
-    w1_grad = jnp.einsum("td,tf->df", mlp_full, grad_pre, preferred_element_type=F32)
     w1_grad = reduce_all(w1_grad, "dp")
-    grad_norm_c = scatter_rel(
-        jnp.einsum("tf,df->td", grad_pre, w1, preferred_element_type=F32).reshape(size, local_rows, width), "mp"
-    )
-    grad_hidden_c, gain_c, shift_c = pull_c(grad_norm_c)
-    grad_hidden = grad_out + grad_hidden_c
-    grad_attn, gain_b, shift_b = pull_b(grad_hidden)
-    attn_grad_low = grad_attn.astype(BF)
-    out_bias_part = jnp.sum(attn_grad_low.astype(F32), axis=0)
-    attn_grad_full = sort(gather_rel(attn_grad_low, "mp"))
-    wout_grad = jnp.einsum("tc,td->cd", head_low, attn_grad_full, preferred_element_type=F32)
     wout_grad = reduce_all(wout_grad, "dp")
-    grad_heads = jnp.einsum("td,cd->tc", attn_grad_full, wout, preferred_element_type=F32).astype(BF)
     grads = attn_bwd(bounds, queries, keys, values, head_low, grad_heads, lse)
     grad_proj = jnp.concatenate(grads, axis=1)
     part_sums = jnp.sum(grad_proj.astype(F32), axis=0).reshape(3, head_part)
@@ -284,9 +679,7 @@
     own_sums = sum_small(jnp.concatenate([qv_part.reshape(-1), b1_grad]), ("dp",))
     qv_sum = own_sums[: 2 * head_part].reshape(2, head_part)
     b1_sum = own_sums[2 * head_part:]
-    stack = jnp.stack(
-        [gain_a, gain_b, gain_c, gain_d, shift_a, shift_b, shift_c, shift_d, out_bias_part, b2_part]
-    )
+    stack = jnp.concatenate([gain_a[None], mid_sums[0:3], shift_a[None], mid_sums[3:8]])
     stack = sum_small(stack, ("mp", "dp"))
     return (
         mixed, tokens_grad, wqkv_grad, qv_sum, wout_grad, stack[8], w1_grad, b1_sum, w2_grad, stack[9],

time: 569 us -> 542 us (0.953)
  Pallas kernels: 60.6 us -> 220 us
  waiting for transfers between devices: 246 us -> 156 us
  matrix products: 61.4 us -> 14 us
  other arithmetic: 94.8 us -> 55.1 us
  local copies, waits for them, and re-layouts: 39.4 us -> 31.3 us
    pallas_call x0 -> x1, Pallas kernels: none -> 160 us  [middle(): pl.pallas_call(mid_kernel, in_specs=[vmem] * 8, out_specs=[vmem, vmem, vm...]
    ppermute x56 -> x38, waiting for transfers between devices: 246 us -> 156 us  [swap(): return lax.ppermute(values, axis, [(i, i ^ mask) for i in range(size)])]
    dot_general x9 -> x0, matrix products: 50 us -> none  [the longest x1 12.5 us: shards(): jnp.einsum('td,fd->tf', branch_full, w2, preferred_element_type=F32)]
    reduce_sum x5 -> x2, other arithmetic: 14.8 us -> 4.21 us  [layer_norm(): return center * lax.rsqrt(spread + eps_norm) * gain + shift]
    select_n x10, other arithmetic: 19.9 us -> 13.6 us  [reduce_all(): low = jnp.where(bit == 0, both, flipped)]
    ppermute x56 -> x38, starting transfers between devices: 54.7 us -> 51.2 us  [swap(): return lax.ppermute(values, axis, [(i, i ^ mask) for i in range(size)])]
    unnamed x112 -> x65, local copies, waits for them, and re-layouts: 13.3 us -> 10.2 us
  transfers between devices with their start and end apart: 56 -> 38, of which waited for: 27 -> 16; matrix products, arithmetic and copies ran while one was open for 23% -> 13% of each run, Pallas kernels for 7% -> 0%
where the time goes in v2:
time: 542 us; the launch traced here: 532 us
  Pallas kernels  220 us (41%)
  waiting for transfers between devices  156 us (29%)
  other arithmetic  55.1 us (10%)
  starting transfers between devices  51.2 us (9%)
  local copies, waits for them, and re-layouts  31.3 us (6%)
  matrix products  14 us (3%)
    pallas_call x1, Pallas kernels, middle(): pl.pallas_call(mid_kernel, in_specs=[vmem] * 8, out_specs=[vmem, vmem, vm...  160 us
    ppermute x38, waiting for transfers between devices, swap(): return lax.ppermute(values, axis, [(i, i ^ mask) for i in range(size)])  156 us
    ppermute x38, starting transfers between devices, swap(): return lax.ppermute(values, axis, [(i, i ^ mask) for i in range(size)])  51.2 us
    pallas_call x1, Pallas kernels, attn_bwd(): pl.pallas_call(bwd_kernel, grid=(H,), in_specs=[pl.BlockSpec(memory_space...  38.3 us
    pallas_call x1, Pallas kernels, attn_fwd(): pl.pallas_call(fwd_kernel, grid=(H,), in_specs=[pl.BlockSpec(memory_space...  21.9 us
    select_n x10, other arithmetic, reduce_all(): low = jnp.where(bit == 0, both, flipped)  13.6 us
    convert_element_type x4, other arithmetic, reduce_all(): return low.astype(F32)  13.5 us
  transfers between devices with their start and end apart: 38, of which 16 were waited for; matrix products, arithmetic and copies ran while one was open for 13% of the time, Pallas kernels for 0%

profile of v2, /device:TPU:0, one launch (start us, length us, event | category | flops | bytes accessed | tf_op | source)
XLA Modules:
  0.0 532.0 jit_solution(17390591631693145588)
XLA Ops:
  5.6 2.9 collective-permute-start.1
  8.6 24.9 %collective-permute-done.1 = bf16[544,1024]{1,0:T(8,128)(2,1)} collective-permute-done((bf16[544,1024]{1,0:T(8,128)(2,1)}, bf16[544,1024]{1,0:T(8,128)(2,1)}, u32[]{:S(2)}, u32[]{:S(2)}) %collective-permute-start.1) | collective-permute-done | bytes 1114144 | tf_op jit(solution)/shard_map/ppermute | solution.py:145
  44.2 3.9 add_convert_fusion
  50.0 21.9 %attn_fwd.1 = (bf16[2176,256]{1,0:T(8,128)(2,1)}, f32[4,8,2176]{2,1,0:T(8,128)}) custom-call(s32[3]{0:T(128)} %pad_add_fusion.bounds, bf16[2176,256]{1,0:T(8,128)(2,1)} %get-tuple-element.57.q_ref, bf16[2176,256]{1,0:T(8,128)(2,1)} %get-tuple-element.56.k_ref, bf16[2176,256]{1,0:T(8,128)(2,1)} %get-tuple-element.55.v_ref), custom_call_target="tpu_custom_call" | custom-call | tf_op jit(solution)/shard_map/attn_fwd/pallas_call | solution.py:114
  71.9 160.1 %middle.1 = (bf16[544,1024]{1,0:T(8,128)(2,1)}, f32[544,1024]{1,0:T(8,128)}, bf16[2176,256]{1,0:T(8,128)(2,1)}, f32[1024,1024]{1,0:T(8,128)}, f32[1024,1024]{1,0...) custom-call(bf16[2176,256]{1,0:T(8,128)(2,1)} %get-tuple-element.25.heads.o_ref, ...), custom_call_target="tpu_custom_call" | custom-call | flops 31943819264 | bytes 41943040 | tf_op jit(solution)/shard_map/middle/pallas_call | solution.py:525
  232.0 38.3 %attn_bwd.1 = (bf16[2176,256]{1,0:T(8,128)(2,1)}, bf16[2176,256]{1,0:T(8,128)(2,1)}, bf16[2176,256]{1,0:T(8,128)(2,1)}) custom-call(s32[3]{0:T(128)} %pad_add_fusion.bounds, bf16[2176,256]{1,0:T(8,128)(2,1)} %get-tuple-element.57.q_ref, bf16[2176,256]{1,0:T(8,128)(2,1)} %get-tuple-element.56.k_ref, bf16[2176,256]{1,0:T(8,128)(2,1)} %get-tuple-element.55.v_ref, ...), custom_call_target="tpu_custom_call" | custom-call | tf_op jit(solution)/shard_map/attn_bwd/pallas_call | solution.py:124
  274.2 3.9 fusion.41
  284.2 3.1 collective-permute-start.12
  291.9 6.2 %fusion.40 = (bf16[4,544,1024]{2,1,0:T(8,128)(2,1)S(1)}, f32[4,544,1024]{2,1,0:T(8,128)}) fusion(bf16[1024,768,1]{0,1,2:T(8,128)(2,1)S(1)} %bitcast.62, bf16[1,544,768]{2,1,0:T(8,128)(2,1)S(1)} %get-tuple-element.52, bf16[1,544,768]{2,1,0:T(8,128)(2,1)S(1)} %get-tuple-element.53, bf16[1,544,768]{2,1,0:T(8,128)(2,1)S(1)} %get-tuple-element.54, ...), kind=kOutput, calls=%fused_computation.111 | convolution fusion | flops 3429793792 | bytes 18284544 | tf_op jit(solution)/shard_map/jtc,dc->jtd/dot_general | solution.py:676
  300.4 3.8 collective-permute-done.17
  310.1 2.7 dynamic-slice_convert_fusion.1
  314.6 13.4 %collective-permute-done.14 = f32[1536]{0:T(1024)S(1)} collective-permute-done((f32[1536]{0:T(1024)S(1)}, f32[1536]{0:T(1024)S(1)}, u32[]{:S(2)}, u32[]{:S(2)}) %collective-permute-start.14) | collective-permute-done | bytes 6176 | tf_op jit(solution)/shard_map/ppermute | solution.py:145
  333.4 22.7 %collective-permute-done.20 = bf16[128,1024]{1,0:T(8,128)(2,1)S(1)} collective-permute-done((bf16[128,1024]{1,0:T(8,128)(2,1)S(1)}, bf16[128,1024]{1,0:T(8,128)(2,1)S(1)}, u32[]{:S(2)}, u32[]{:S(2)}) %collective-permute-start.20) | collective-permute-done | bytes 262176 | tf_op jit(solution)/shard_map/ppermute | solution.py:145
  365.0 3.1 collective-permute-done.7
  368.3 3.1 collective-permute-start.8
  371.3 3.0 fusion.20
  375.9 17.4 %collective-permute-done.8 = bf16[128,768]{0,1:T(8,128)(2,1)S(1)} collective-permute-done((bf16[128,768]{0,1:T(8,128)(2,1)S(1)}, bf16[128,768]{0,1:T(8,128)(2,1)S(1)}, u32[]{:S(2)}, u32[]{:S(2)}) %collective-permute-start.8) | collective-permute-done | bytes 196640 | tf_op jit(solution)/shard_map/ppermute | solution.py:145
  393.3 3.4 collective-permute-start.9
  400.5 3.0 collective-permute-start.28
  403.5 14.6 %collective-permute-done.9 = bf16[128,768]{0,1:T(8,128)(2,1)} collective-permute-done((bf16[128,768]{0,1:T(8,128)(2,1)S(1)}, bf16[128,768]{0,1:T(8,128)(2,1)}, u32[]{:S(2)}, u32[]{:S(2)}) %collective-permute-start.9) | collective-permute-done | bytes 196640 | tf_op jit(solution)/shard_map/ppermute | solution.py:145
  420.5 3.3 collective-permute-done.34
  426.0 6.1 %collective-permute-done.28 = bf16[128,1024]{1,0:T(8,128)(2,1)S(1)} collective-permute-done((bf16[128,1024]{1,0:T(8,128)(2,1)S(1)}, bf16[128,1024]{1,0:T(8,128)(2,1)S(1)}, u32[]{:S(2)}, u32[]{:S(2)}) %collective-permute-start.28) | collective-permute-done | bytes 262176 | tf_op jit(solution)/shard_map/ppermute | solution.py:145
  432.3 11.1 %collective-permute-done.35 = bf16[128,1024]{1,0:T(8,128)(2,1)S(1)} collective-permute-done((bf16[128,1024]{1,0:T(8,128)(2,1)S(1)}, bf16[128,1024]{1,0:T(8,128)(2,1)S(1)}, u32[]{:S(2)}, u32[]{:S(2)}) %collective-permute-start.35) | collective-permute-done | bytes 262176 | tf_op jit(solution)/shard_map/ppermute | solution.py:145
  446.3 3.1 fusion.18
  460.3 3.4 collective-permute-start.23
  468.2 4.9 collective-permute-start.24
  476.9 2.9 maximum_select_fusion.3
  480.3 3.0 maximum_select_fusion.4
  492.2 14.1 %collective-permute-done.31 = bf16[512,1024]{1,0:T(8,128)(2,1)} collective-permute-done((bf16[512,1024]{1,0:T(8,128)(2,1)}, bf16[512,1024]{1,0:T(8,128)(2,1)}, u32[]{:S(2)}, u32[]{:S(2)}) %collective-permute-start.31) | collective-permute-done | bytes 1048608 | tf_op jit(solution)/shard_map/ppermute | solution.py:145
  506.2 5.3 fusion.23
  511.5 13.9 %collective-permute-done.37 = bf16[512,1024]{1,0:T(8,128)(2,1)} collective-permute-done((bf16[512,1024]{1,0:T(8,128)(2,1)}, bf16[512,1024]{1,0:T(8,128)(2,1)}, u32[]{:S(2)}, u32[]{:S(2)}) %collective-permute-start.37) | collective-permute-done | bytes 1048608 | tf_op jit(solution)/shard_map/ppermute | solution.py:145
  525.4 5.2 fusion.24
  (206 shorter events, 96.3 us)
Async XLA Ops:
  5.6 27.8 %collective-permute-start.1 = (bf16[544,1024]{1,0:T(8,128)(2,1)}, bf16[544,1024]{1,0:T(8,128)(2,1)}, u32[]{:S(2)}, u32[]{:S(2)}) collective-permute-start(bf16[544,1024]{1,0:T(8,128)(2,1)} %fusion.15), channel_id=1, source_target_pairs={{0,2},{1,3},{2,0},{3,1},{4,6},{5,7},{6,4},{7,5},{8,10},{9,11},{10,... | collective-permute-start | bytes 3342344 | tf_op jit(solution)/shard_map/ppermute | solution.py:145
  8.5 31.6 %collective-permute-start = (bf16[544,1024]{1,0:T(8,128)(2,1)}, bf16[544,1024]{1,0:T(8,128)(2,1)}, u32[]{:S(2)}, u32[]{:S(2)}) collective-permute-start(bf16[544,1024]{1,0:T(8,128)(2,1)} %fusion.15), channel_id=1, source_target_pairs={{0,1},{1,0},{2,3},{3,2},{4,5},{5,4},{6,7},{7,6},{8,9},{9,8},{10,11... | collective-permute-start | bytes 3342344 | tf_op jit(solution)/shard_map/ppermute | solution.py:145
  279.4 10.8 %collective-permute-start.15 = (bf16[128,1024]{1,0:T(8,128)(2,1)S(1)}, bf16[128,1024]{1,0:T(8,128)(2,1)S(1)}, u32[]{:S(2)}, u32[]{:S(2)}) collective-permute-start(bf16[128,1024]{1,0:T(8,128)(2,1)S(1)} %dynamic-slice_convert_fusion.8), channel_id=1, source_target_pairs={{0,4},{4,0},{8,12},{12,8},{16,20},{20,16},{24,28},{28,24},{1,5},{5... | collective-permute-start | bytes 786440 | tf_op jit(solution)/shard_map/ppermute | solution.py:145
  284.2 75.0 %collective-permute-start.32 = (bf16[512,1024]{1,0:T(8,128)(2,1)}, bf16[512,1024]{1,0:T(8,128)(2,1)}, u32[]{:S(2)}, u32[]{:S(2)}) collective-permute-start(bf16[512,1024]{1,0:T(8,128)(2,1)} %dynamic-slice_convert_fusion), channel_id=1, source_target_pairs={{0,4},{4,0},{8,12},{12,8},{16,20},{20,16},{24,28},{28,24},{1,5},{5... | collective-permute-start | bytes 3145736 | tf_op jit(solution)/shard_map/ppermute | solution.py:145
  284.2 15.6 %collective-permute-start.12 = (f32[1536]{0:T(1024)S(1)}, f32[1536]{0:T(1024)S(1)}, u32[]{:S(2)}, u32[]{:S(2)}) collective-permute-start(f32[1536]{0:T(1024)S(1)} %pad_maximum_fusion.3), channel_id=1, source_target_pairs={{0,16},{4,20},{8,24},{12,28},{16,0},{20,4},{24,8},{28,12},{1,17},{... | collective-permute-start | bytes 18440 | tf_op jit(solution)/shard_map/ppermute | solution.py:145
  288.4 41.4 %collective-permute-start.6 = (bf16[512,768]{0,1:T(8,128)(2,1)}, bf16[512,768]{0,1:T(8,128)(2,1)}, u32[]{:S(2)}, u32[]{:S(2)}) collective-permute-start(bf16[512,768]{0,1:T(8,128)(2,1)} %dynamic-slice_convert_fusion.2), channel_id=1, source_target_pairs={{0,4},{4,0},{8,12},{12,8},{16,20},{20,16},{24,28},{28,24},{1,5},{5... | collective-permute-start | bytes 2359304 | tf_op jit(solution)/shard_map/ppermute | solution.py:145
  290.2 7.9 %collective-permute-start.16 = (bf16[64,1024]{1,0:T(8,128)(2,1)S(1)}, bf16[64,1024]{1,0:T(8,128)(2,1)S(1)}, u32[]{:S(2)}, u32[]{:S(2)}) collective-permute-start(bf16[64,1024]{1,0:T(8,128)(2,1)S(1)} %dynamic-slice_convert_fusion.10), channel_id=1, source_target_pairs={{0,8},{4,12},{8,0},{12,4},{16,24},{20,28},{24,16},{28,20},{1,9},{5... | collective-permute-start | bytes 393224 | tf_op jit(solution)/shard_map/ppermute | solution.py:145
  306.6 21.4 %collective-permute-start.14 = (f32[1536]{0:T(1024)S(1)}, f32[1536]{0:T(1024)S(1)}, u32[]{:S(2)}, u32[]{:S(2)}) collective-permute-start(f32[1536]{0:T(1024)S(1)} %add.247), channel_id=1, source_target_pairs={{0,4},{4,0},{8,12},{12,8},{16,20},{20,16},{24,28},{28,24},{1,5},{5... | collective-permute-start | bytes 18440 | tf_op jit(solution)/shard_map/ppermute | solution.py:145
  310.1 19.6 %collective-permute-start.19 = (bf16[64,1024]{1,0:T(8,128)(2,1)S(1)}, bf16[64,1024]{1,0:T(8,128)(2,1)S(1)}, u32[]{:S(2)}, u32[]{:S(2)}) collective-permute-start(bf16[64,1024]{1,0:T(8,128)(2,1)S(1)} %maximum_select_fusion.13), channel_id=1, source_target_pairs={{0,8},{4,12},{8,0},{12,4},{16,24},{20,28},{24,16},{28,20},{1,9},{5... | collective-permute-start | bytes 393224 | tf_op jit(solution)/shard_map/ppermute | solution.py:145
  314.1 47.2 %collective-permute-start.26 = (bf16[512,1024]{1,0:T(8,128)(2,1)}, bf16[512,1024]{1,0:T(8,128)(2,1)}, u32[]{:S(2)}, u32[]{:S(2)}) collective-permute-start(bf16[512,1024]{1,0:T(8,128)(2,1)} %dynamic-slice_convert_fusion.1), channel_id=1, source_target_pairs={{0,4},{4,0},{8,12},{12,8},{16,20},{20,16},{24,28},{28,24},{1,5},{5... | collective-permute-start | bytes 3145736 | tf_op jit(solution)/shard_map/ppermute | solution.py:145
  328.0 118.2 %collective-permute-start.3 = (bf16[544,1024]{1,0:T(8,128)(2,1)}, bf16[544,1024]{1,0:T(8,128)(2,1)}, u32[]{:S(2)}, u32[]{:S(2)}) collective-permute-start(bf16[544,1024]{1,0:T(8,128)(2,1)} %get-tuple-element.45), channel_id=1, source_target_pairs={{0,1},{1,0},{2,3},{3,2},{4,5},{5,4},{6,7},{7,6},{8,9},{9,8},{10,11... | collective-permute-start | bytes 3342344 | tf_op jit(solution)/shard_map/ppermute | solution.py:145
  329.6 41.7 %collective-permute-start.4 = (bf16[544,1024]{1,0:T(8,128)(2,1)}, bf16[544,1024]{1,0:T(8,128)(2,1)S(1)}, u32[]{:S(2)}, u32[]{:S(2)}) collective-permute-start(bf16[544,1024]{1,0:T(8,128)(2,1)} %get-tuple-element.46), channel_id=1, source_target_pairs={{0,1},{1,0},{2,3},{3,2},{4,5},{5,4},{6,7},{7,6},{8,9},{9,8},{10,11... | collective-permute-start | bytes 3342344 | tf_op jit(solution)/shard_map/ppermute | solution.py:145
  329.8 26.3 %collective-permute-start.20 = (bf16[128,1024]{1,0:T(8,128)(2,1)S(1)}, bf16[128,1024]{1,0:T(8,128)(2,1)S(1)}, u32[]{:S(2)}, u32[]{:S(2)}) collective-permute-start(bf16[128,1024]{1,0:T(8,128)(2,1)S(1)} %maximum_select_fusion.12), channel_id=1, source_target_pairs={{0,4},{4,0},{8,12},{12,8},{16,20},{20,16},{24,28},{28,24},{1,5},{5... | collective-permute-start | bytes 786440 | tf_op jit(solution)/shard_map/ppermute | solution.py:145
  356.1 12.0 %collective-permute-start.7 = (bf16[256,768]{0,1:T(8,128)(2,1)S(1)}, bf16[256,768]{0,1:T(8,128)(2,1)S(1)}, u32[]{:S(2)}, u32[]{:S(2)}) collective-permute-start(bf16[256,768]{0,1:T(8,128)(2,1)S(1)} %dynamic-slice_convert_fusion.5), channel_id=1, source_target_pairs={{0,8},{4,12},{8,0},{12,4},{16,24},{20,28},{24,16},{28,20},{1,9},{5... | collective-permute-start | bytes 1179656 | tf_op jit(solution)/shard_map/ppermute | solution.py:145
  361.1 35.8 %collective-permute-start.33 = (bf16[256,1024]{1,0:T(8,128)(2,1)S(1)}, bf16[256,1024]{1,0:T(8,128)(2,1)}, u32[]{:S(2)}, u32[]{:S(2)}) collective-permute-start(bf16[256,1024]{1,0:T(8,128)(2,1)S(1)} %dynamic-slice_convert_fusion.3), channel_id=1, source_target_pairs={{0,8},{4,12},{8,0},{12,4},{16,24},{20,28},{24,16},{28,20},{1,9},{5... | collective-permute-start | bytes 1572872 | tf_op jit(solution)/shard_map/ppermute | solution.py:145
  363.4 35.8 %collective-permute-start.27 = (bf16[256,1024]{1,0:T(8,128)(2,1)S(1)}, bf16[256,1024]{1,0:T(8,128)(2,1)}, u32[]{:S(2)}, u32[]{:S(2)}) collective-permute-start(bf16[256,1024]{1,0:T(8,128)(2,1)S(1)} %dynamic-slice_convert_fusion.4), channel_id=1, source_target_pairs={{0,8},{4,12},{8,0},{12,4},{16,24},{20,28},{24,16},{28,20},{1,9},{5... | collective-permute-start | bytes 1572872 | tf_op jit(solution)/shard_map/ppermute | solution.py:145
  368.3 25.0 %collective-permute-start.8 = (bf16[128,768]{0,1:T(8,128)(2,1)S(1)}, bf16[128,768]{0,1:T(8,128)(2,1)S(1)}, u32[]{:S(2)}, u32[]{:S(2)}) collective-permute-start(bf16[128,768]{0,1:T(8,128)(2,1)S(1)} %dynamic-slice_convert_fusion.9), channel_id=1, source_target_pairs={{0,16},{4,20},{8,24},{12,28},{16,0},{20,4},{24,8},{28,12},{1,17},{... | collective-permute-start | bytes 589832 | tf_op jit(solution)/shard_map/ppermute | solution.py:145
  374.4 71.9 %collective-permute-start.5 = (bf16[544,1024]{1,0:T(8,128)(2,1)}, bf16[544,1024]{1,0:T(8,128)(2,1)}, u32[]{:S(2)}, u32[]{:S(2)}) collective-permute-start(bf16[544,1024]{1,0:T(8,128)(2,1)} %fusion.20), channel_id=1, source_target_pairs={{0,2},{1,3},{2,0},{3,1},{4,6},{5,7},{6,4},{7,5},{8,10},{9,11},{10,... | collective-permute-start | bytes 3342344 | tf_op jit(solution)/shard_map/ppermute | solution.py:145
  393.3 24.8 %collective-permute-start.9 = (bf16[128,768]{0,1:T(8,128)(2,1)S(1)}, bf16[128,768]{0,1:T(8,128)(2,1)}, u32[]{:S(2)}, u32[]{:S(2)}) collective-permute-start(bf16[128,768]{0,1:T(8,128)(2,1)S(1)} %add_convert_fusion.4), channel_id=1, source_target_pairs={{0,16},{4,20},{8,24},{12,28},{16,0},{20,4},{24,8},{28,12},{1,17},{... | collective-permute-start | bytes 589832 | tf_op jit(solution)/shard_map/ppermute | solution.py:145
  399.2 24.6 %collective-permute-start.34 = (bf16[128,1024]{1,0:T(8,128)(2,1)}, bf16[128,1024]{1,0:T(8,128)(2,1)}, u32[]{:S(2)}, u32[]{:S(2)}) collective-permute-start(bf16[128,1024]{1,0:T(8,128)(2,1)} %dynamic-slice_convert_fusion.6), channel_id=1, source_target_pairs={{0,16},{4,20},{8,24},{12,28},{16,0},{20,4},{24,8},{28,12},{1,17},{... | collective-permute-start | bytes 786440 | tf_op jit(solution)/shard_map/ppermute | solution.py:145
  400.5 31.6 %collective-permute-start.28 = (bf16[128,1024]{1,0:T(8,128)(2,1)S(1)}, bf16[128,1024]{1,0:T(8,128)(2,1)S(1)}, u32[]{:S(2)}, u32[]{:S(2)}) collective-permute-start(bf16[128,1024]{1,0:T(8,128)(2,1)S(1)} %dynamic-slice_convert_fusion.7), channel_id=1, source_target_pairs={{0,16},{4,20},{8,24},{12,28},{16,0},{20,4},{24,8},{28,12},{1,17},{... | collective-permute-start | bytes 786440 | tf_op jit(solution)/shard_map/ppermute | solution.py:145
  420.4 34.6 %collective-permute-start.10 = (bf16[256,768]{0,1:T(8,128)(2,1)S(1)}, bf16[256,768]{0,1:T(8,128)(2,1)S(1)}, u32[]{:S(2)}, u32[]{:S(2)}) collective-permute-start(bf16[256,768]{0,1:T(8,128)(2,1)S(1)} %maximum_select_fusion.11), channel_id=1, source_target_pairs={{0,8},{4,12},{8,0},{12,4},{16,24},{20,28},{24,16},{28,20},{1,9},{5... | collective-permute-start | bytes 1179656 | tf_op jit(solution)/shard_map/ppermute | solution.py:145
  425.0 18.3 %collective-permute-start.35 = (bf16[128,1024]{1,0:T(8,128)(2,1)S(1)}, bf16[128,1024]{1,0:T(8,128)(2,1)S(1)}, u32[]{:S(2)}, u32[]{:S(2)}) collective-permute-start(bf16[128,1024]{1,0:T(8,128)(2,1)S(1)} %add_convert_fusion.2), channel_id=1, source_target_pairs={{0,16},{4,20},{8,24},{12,28},{16,0},{20,4},{24,8},{28,12},{1,17},{... | collective-permute-start | bytes 786440 | tf_op jit(solution)/shard_map/ppermute | solution.py:145
  432.2 20.0 %collective-permute-start.29 = (bf16[128,1024]{1,0:T(8,128)(2,1)S(1)}, bf16[128,1024]{1,0:T(8,128)(2,1)S(1)}, u32[]{:S(2)}, u32[]{:S(2)}) collective-permute-start(bf16[128,1024]{1,0:T(8,128)(2,1)S(1)} %add_convert_fusion.3), channel_id=1, source_target_pairs={{0,16},{4,20},{8,24},{12,28},{16,0},{20,4},{24,8},{28,12},{1,17},{... | collective-permute-start | bytes 786440 | tf_op jit(solution)/shard_map/ppermute | solution.py:145
  444.3 36.1 %collective-permute-start.36 = (bf16[256,1024]{1,0:T(8,128)(2,1)}, bf16[256,1024]{1,0:T(8,128)(2,1)}, u32[]{:S(2)}, u32[]{:S(2)}) collective-permute-start(bf16[256,1024]{1,0:T(8,128)(2,1)} %maximum_select_fusion.9), channel_id=1, source_target_pairs={{0,8},{4,12},{8,0},{12,4},{16,24},{20,28},{24,16},{28,20},{1,9},{5... | collective-permute-start | bytes 1572872 | tf_op jit(solution)/shard_map/ppermute | solution.py:145
  453.1 23.8 %collective-permute-start.30 = (bf16[256,1024]{1,0:T(8,128)(2,1)}, bf16[256,1024]{1,0:T(8,128)(2,1)}, u32[]{:S(2)}, u32[]{:S(2)}) collective-permute-start(bf16[256,1024]{1,0:T(8,128)(2,1)} %maximum_select_fusion.8), channel_id=1, source_target_pairs={{0,8},{4,12},{8,0},{12,4},{16,24},{20,28},{24,16},{28,20},{1,9},{5... | collective-permute-start | bytes 1572872 | tf_op jit(solution)/shard_map/ppermute | solution.py:145
  458.8 29.1 %collective-permute-start.11 = (bf16[512,768]{0,1:T(8,128)(2,1)}, bf16[512,768]{0,1:T(8,128)(2,1)S(1)}, u32[]{:S(2)}, u32[]{:S(2)}) collective-permute-start(bf16[512,768]{0,1:T(8,128)(2,1)} %maximum_select_fusion.6), channel_id=1, source_target_pairs={{0,4},{4,0},{8,12},{12,8},{16,20},{20,16},{24,28},{28,24},{1,5},{5... | collective-permute-start | bytes 2359304 | tf_op jit(solution)/shard_map/ppermute | solution.py:145
  460.3 7.8 %collective-permute-start.23 = (f32[10,1024]{1,0:T(8,128)S(1)}, f32[10,1024]{1,0:T(8,128)S(1)}, u32[]{:S(2)}, u32[]{:S(2)}) collective-permute-start(f32[10,1024]{1,0:T(8,128)S(1)} %add.259), channel_id=1, source_target_pairs={{0,16},{4,20},{8,24},{12,28},{16,0},{20,4},{24,8},{28,12},{1,17},{... | collective-permute-start | bytes 122888 | tf_op jit(solution)/shard_map/ppermute | solution.py:145
  468.2 7.1 %collective-permute-start.24 = (f32[10,1024]{1,0:T(8,128)S(1)}, f32[10,1024]{1,0:T(8,128)S(1)}, u32[]{:S(2)}, u32[]{:S(2)}) collective-permute-start(f32[10,1024]{1,0:T(8,128)S(1)} %add.260), channel_id=1, source_target_pairs={{0,8},{4,12},{8,0},{12,4},{16,24},{20,28},{24,16},{28,20},{1,9},{5... | collective-permute-start | bytes 122888 | tf_op jit(solution)/shard_map/ppermute | solution.py:145
  475.3 11.3 %collective-permute-start.25 = (f32[10,1024]{1,0:T(8,128)S(1)}, f32[10,1024]{1,0:T(8,128)S(1)}, u32[]{:S(2)}, u32[]{:S(2)}) collective-permute-start(f32[10,1024]{1,0:T(8,128)S(1)} %add.261), channel_id=1, source_target_pairs={{0,4},{4,0},{8,12},{12,8},{16,20},{20,16},{24,28},{28,24},{1,5},{5... | collective-permute-start | bytes 122888 | tf_op jit(solution)/shard_map/ppermute | solution.py:145
  479.8 26.4 %collective-permute-start.31 = (bf16[512,1024]{1,0:T(8,128)(2,1)}, bf16[512,1024]{1,0:T(8,128)(2,1)}, u32[]{:S(2)}, u32[]{:S(2)}) collective-permute-start(bf16[512,1024]{1,0:T(8,128)(2,1)} %maximum_select_fusion.3), channel_id=1, source_target_pairs={{0,4},{4,0},{8,12},{12,8},{16,20},{20,16},{24,28},{28,24},{1,5},{5... | collective-permute-start | bytes 3145736 | tf_op jit(solution)/shard_map/ppermute | solution.py:145
  483.3 42.0 %collective-permute-start.37 = (bf16[512,1024]{1,0:T(8,128)(2,1)}, bf16[512,1024]{1,0:T(8,128)(2,1)}, u32[]{:S(2)}, u32[]{:S(2)}) collective-permute-start(bf16[512,1024]{1,0:T(8,128)(2,1)} %maximum_select_fusion.4), channel_id=1, source_target_pairs={{0,4},{4,0},{8,12},{12,8},{16,20},{20,16},{24,28},{28,24},{1,5},{5... | collective-permute-start | bytes 3145736 | tf_op jit(solution)/shard_map/ppermute | solution.py:145
  (36 other events, 389.1 us)
